TPU v7x, 32 devices: a whole 2x2x4 slice. The times are simulated.
32 devices in a mesh: lat: 4 (over x, core), lon: 8 (over z, y).
Axes of the slice: x: 2, y: 2, z: 4, core: 2. Of those that a mesh axis runs over, the one named last changes fastest.
Arguments:
- latent: bfloat16 [32, 2048, 128], P('lat', 'lon'), may hold values from -6 to 6
- head: bfloat16 [128, 32], replicated, may hold values from -0.5 to 0.5
- bias: float32 [32], replicated, may hold values from -3 to 3
- targets: bfloat16 [32, 32, 1024], P(None, 'lat', 'lon'), may hold values from -6 to 6
- margin_cell: int32 [4, 8, 6144], P('lat', 'lon'), may hold values from 0 to 2047
- margin_pixel: int32 [4, 8, 6144], P('lat', 'lon'), may hold values from 0 to 2047, as said below
- margin_weight: float32 [4, 8, 6144], P('lat', 'lon'), may hold values from 0.05 to 1
- live_count: int32 [4, 8], P('lat', 'lon'), may hold values from 2457 to 6144, as said below
Outputs:
- latent_grad: bfloat16 [32, 2048, 128], P('lat', 'lon')
- head_grad: float32 [128, 32], replicated
- bias_grad: float32 [32], replicated
Inputs may be any that keep to these rules, and one draw needn't show every extreme that they name: `margin_pixel`: A tile pixel in the device's own band: tile row times (256) plus q, where q - 64 is the column relative to the device's own sector, so q < 64 and q >= 192 are the neighbouring sectors' columns. Both 0 and the largest value occur in every device's list; columns near the frame's edges are covered thinly or not at all. `live_count`: rows at or beyond a device's count are padding and are ignored; in every draw some device has all 6144 rows live.
All inputs are finite; a program needn't handle non-finite values.
Results may differ from a plain program's by a relative error of at most 0.0052.
Values may be sent and summed in bfloat16 or wider, within the bound.
No kernel may reach another device: no remote copies, remote signals or barrier semaphores. Data moves between devices by JAX's collectives and lax.ppermute only.
A program may use at most 64 MiB of HBM per device.

v0:
```python
import math

import jax
import jax.numpy as jnp
from jax import lax
from jax.sharding import PartitionSpec as P


def from_behind(shard, axis, by):
    devices = lax.axis_size(axis)
    return lax.ppermute(shard, axis, [(i, (i + by) % devices) for i in range(devices)])


def with_halo(cells, sides, width):
    for axis, dim in sides:
        count = lax.axis_size(axis)
        head = lax.slice_in_dim(cells, 0, width, axis=dim)
        tail = lax.slice_in_dim(cells, cells.shape[dim] - width, cells.shape[dim], axis=dim)
        cells = jnp.concatenate(
            [
                lax.ppermute(tail, axis, [(i, (i + 1) % count) for i in range(count)]),
                cells,
                lax.ppermute(head, axis, [((i + 1) % count, i) for i in range(count)]),
            ],
            axis=dim,
        )
    return cells


def accumulate(step_fn, initial, row_total):
    return step_fn(initial, 0, row_total)


def per_device(latent, head, bias, targets, margin_cell, margin_pixel, margin_weight, live_count):
    cycle_count, cycle_cells, latent_width = latent.shape
    cell_total = cycle_count * cycle_cells
    latent_rows = latent.reshape(cell_total, latent_width)
    var_count, tile_rows, tile_cols = targets.shape
    rim_width = tile_cols // 2
    frame_width = tile_cols + 2 * rim_width
    cell_ids = margin_cell.reshape(-1)
    pixel_ids = margin_pixel.reshape(-1)
    row_total = cell_ids.shape[0]
    live_total = live_count.reshape(())
    row_index = jnp.arange(row_total, dtype=jnp.int32)
    live_weight = jnp.where(row_index < live_total, margin_weight.reshape(-1), jnp.float32(0.0))
    predicted = (
        lax.dot_general(
            head, latent_rows, (((0,), (1,)), ((), ())), preferred_element_type=jnp.float32
        )
        + bias[:, None]
    ).astype(jnp.bfloat16)

    def spread(totals, first_row, row_span):
        contribution = (
            jnp.take(predicted, cell_ids, axis=1).astype(jnp.float32) * live_weight[None, :]
        )
        return totals.at[:, pixel_ids].add(contribution)

    frame_totals = accumulate(
        spread, jnp.zeros((var_count, tile_rows * frame_width), jnp.float32), row_total
    )
    frame = frame_totals.reshape(var_count, tile_rows, frame_width)
    west_strip = frame[:, :, :rim_width]
    own_part = frame[:, :, rim_width : rim_width + tile_cols]
    east_strip = frame[:, :, rim_width + tile_cols :]
    from_east = from_behind(west_strip, "lon", -1)
    from_west = from_behind(east_strip, "lon", 1)
    own_tiles = own_part.at[:, :, tile_cols - rim_width :].add(from_east)
    own_tiles = own_tiles.at[:, :, :rim_width].add(from_west)
    misfit = own_tiles - targets.astype(jnp.float32)
    misfit_frame = with_halo(misfit, (("lon", 2),), rim_width)
    misfit_flat = misfit_frame.reshape(var_count, tile_rows * frame_width)

    def gather_back(totals, first_row, row_span):
        contribution = jnp.take(misfit_flat, pixel_ids, axis=1) * live_weight[None, :]
        return totals.at[:, cell_ids].add(contribution)

    cell_totals = accumulate(
        gather_back, jnp.zeros((var_count, cell_total), jnp.float32), row_total
    )
    cell_misfit = cell_totals.astype(jnp.bfloat16)
    latent_grad = lax.dot_general(
        cell_misfit, head, (((0,), (1,)), ((), ())), preferred_element_type=jnp.float32
    ).astype(jnp.bfloat16)
    head_part = lax.dot_general(
        latent_rows, cell_misfit, (((0,), (1,)), ((), ())), preferred_element_type=jnp.float32
    )
    bias_part = jnp.sum(cell_misfit.astype(jnp.float32), axis=1)
    head_total, bias_total = lax.psum((head_part, bias_part), ("lat", "lon"))
    grad_scale = 1.0 / math.sqrt(cell_total * lax.axis_size("lat") * lax.axis_size("lon"))
    return (
        latent_grad.reshape(cycle_count, cycle_cells, latent_width),
        head_total * grad_scale,
        bias_total * grad_scale,
    )


def solution(mesh):
    in_specs = (
        P("lat", "lon", None),
        P(),
        P(),
        P(None, "lat", "lon"),
        P("lat", "lon", None),
        P("lat", "lon", None),
        P("lat", "lon", None),
        P("lat", "lon"),
    )
    out_specs = (P("lat", "lon", None), P(), P())
    return jax.shard_map(
        per_device, mesh=mesh, in_specs=in_specs, out_specs=out_specs, check_vma=False
    )
```

profile of v0, /device:TPU:0, one launch (start us, length us, event | category | flops | bytes accessed | tf_op | source)
XLA Modules:
  0.0 179.4 jit_solution(13778949230793606236)
XLA Ops:
  1.4 0.8 compare_select_fusion.1
  2.1 0.8 compare_and_fusion
  2.9 0.8 compare_select_fusion
  3.7 1.0 fusion.6
  4.7 0.3 copy.17
  5.0 56.4 %scatter_custom_fusion = f32[32,2048]{0,1:T(8,128)S(1)} fusion(s32[6144]{0:T(1024)S(1)} %bitcast.29, f32[6144]{0:T(1024)S(1)} %fusion.16, pred[6144]{0:T(1024)(128)(4,1)S(1)} %compare_and_fusion, bf16[]{:T(256)} %constant.87.clone.1, f32[]{:T(128)} %constant.83.clone.1, bf16[32,2048]{0,1:T(8,128)(2,1)S(1)} %copy.17, s32[6144]{0:T(1024)S(1)} %broadcast_clamp_fusion.1), kind=kCustom, calls=%fused_computation.4 | custom fusion | flops 786432 | bytes 841734 | tf_op jit(solution)/shard_map/scatter-add | solution.py:58
  61.4 0.1 fusion.21
  61.5 0.1 copy.25
  61.6 6.1 %collective-permute-start = (f32[32,8,64]{2,1,0:T(8,128)S(1)}, f32[32,8,64]{2,1,0:T(8,128)S(1)}, u32[]{:S(2)}, u32[]{:S(2)}) collective-permute-start(f32[32,8,64]{2,1,0:T(8,128)S(1)} %copy.25), channel_id=1, source_target_pairs={{0,7},{1,0},{2,1},{3,2},{4,3},{5,4},{6,5},{7,6},{8,15},{9,8},{10,9... | collective-permute-start | bytes 196616 | tf_op jit(solution)/shard_map/ppermute | solution.py:11
  67.7 0.1 copy.26
  67.8 0.1 collective-permute-start.1
  68.0 0.2 copy.23
  68.2 0.1 copy.24
  68.3 2.1 %collective-permute-done = f32[32,8,64]{2,1,0:T(8,128)S(1)} collective-permute-done((f32[32,8,64]{2,1,0:T(8,128)S(1)}, f32[32,8,64]{2,1,0:T(8,128)S(1)}, u32[]{:S(2)}, u32[]{:S(2)}) %collective-permute-start) | collective-permute-done | bytes 65568 | tf_op jit(solution)/shard_map/ppermute | solution.py:11
  70.5 4.8 %scatter-add.25 = f32[32,8,128]{2,1,0:T(8,128)S(1)} dynamic-update-slice(f32[32,8,128]{2,1,0:T(8,128)S(1)} %copy.23, f32[32,8,64]{2,1,0:T(8,128)S(1)} %add.72, s32[]{:T(128)} %constant.84.clone.1, s32[]{:T(128)} %constant.84.clone.1, s32[]{:T(128)} %constant.88.clone.1) | dynamic-update-slice | bytes 131076 | tf_op jit(solution)/shard_map/scatter-add | solution.py:69
  75.2 0.3 collective-permute-done.1
  75.6 0.5 scatter-add.26
  76.1 0.1 fusion.22
  76.2 0.2 collective-permute-start.2
  76.3 5.0 %collective-permute-start.3 = (f32[32,8,64]{2,1,0:T(8,128)S(1)}, f32[32,8,64]{2,1,0:T(8,128)S(1)}, u32[]{:S(2)}, u32[]{:S(2)}) collective-permute-start(f32[32,8,64]{2,1,0:T(8,128)S(1)} %get-tuple-element.33), channel_id=1, source_target_pairs={{1,0},{2,1},{3,2},{4,3},{5,4},{6,5},{7,6},{0,7},{9,8},{10,9},{11,1... | collective-permute-start | bytes 196616 | tf_op jit(solution)/shard_map/ppermute | solution.py:23
  81.3 2.9 %collective-permute-done.2 = f32[32,8,64]{2,1,0:T(8,128)S(1)} collective-permute-done((f32[32,8,64]{2,1,0:T(8,128)S(1)}, f32[32,8,64]{2,1,0:T(8,128)S(1)}, u32[]{:S(2)}, u32[]{:S(2)}) %collective-permute-start.2) | collective-permute-done | bytes 65568 | tf_op jit(solution)/shard_map/ppermute | solution.py:21
  84.2 0.9 collective-permute-done.3
  85.1 0.2 pad_maximum_fusion
  85.3 0.4 copy.22
  85.7 51.0 %scatter_custom_fusion.1 = f32[32,2048]{0,1:T(8,128)S(1)} fusion(s32[6144]{0:T(1024)S(1)} %bitcast.28, f32[6144]{0:T(1024)S(1)} %fusion.16, f32[]{:T(128)} %constant.89.clone.1, pred[6144]{0:T(1024)(128)(4,1)S(1)} %compare_and_fusion.1, f32[]{:T(128)} %constant.83.clone.1, f32[32,2048]{0,1:T(8,128)S(1)} %bitcast.25, s32[6144]{0:T(1024)S(1)} %broadcast_clamp_fusion), kind=kCustom, calls=%fused_computation.6 | custom fusion | flops 589824 | bytes 1366024 | tf_op jit(solution)/shard_map/scatter-add | solution.py:77
  136.7 0.3 convert_reduce_fusion
  137.0 0.3 convolution_bitcast_fusion
  137.3 0.4 copy-done.3
  137.7 1.1 convolution_convert_fusion
  138.7 39.5 %all-reduce = (f32[128,32]{0,1:T(8,128)S(1)}, f32[32]{0:T(128)S(1)}) all-reduce(f32[128,32]{0,1:T(8,128)S(1)} %convolution_bitcast_fusion, f32[32]{0:T(128)S(1)} %convert_reduce_fusion), channel_id=1, replica_groups=mesh['lat'=4,'lon'=8] {'lat','lon'}, use_global_device_ids=true, to_apply=%region_2.3 | all-reduce | flops 4128 | bytes 33024 | tf_op jit(solution)/shard_map/psum | solution.py:90
  178.3 0.6 broadcast_multiply_fusion
  178.9 0.5 broadcast_multiply_fusion.1
  (17 shorter events, 0.1 us)
Async XLA Ops:
  0.6 3.0 %copy-start = (bf16[8,256,128]{2,1,0:T(8,128)(2,1)S(1)}, bf16[8,256,128]{2,1,0:T(8,128)(2,1)}, u32[]{:S(2)}) copy-start(bf16[8,256,128]{2,1,0:T(8,128)(2,1)} %param.12) | copy-start | bytes 1572868
  0.6 4.3 %copy-start.4 = (f32[1,1,6144]{2,1,0:T(1,128)S(1)}, f32[1,1,6144]{2,1,0:T(1,128)}, u32[]{:S(2)}) copy-start(f32[1,1,6144]{2,1,0:T(1,128)} %param.18) | copy-start | bytes 73732
  61.6 8.8 %collective-permute-start = (f32[32,8,64]{2,1,0:T(8,128)S(1)}, f32[32,8,64]{2,1,0:T(8,128)S(1)}, u32[]{:S(2)}, u32[]{:S(2)}) collective-permute-start(f32[32,8,64]{2,1,0:T(8,128)S(1)} %copy.25), channel_id=1, source_target_pairs={{0,7},{1,0},{2,1},{3,2},{4,3},{5,4},{6,5},{7,6},{8,15},{9,8},{10,9... | collective-permute-start | bytes 196616 | tf_op jit(solution)/shard_map/ppermute | solution.py:11
  67.8 7.7 %collective-permute-start.1 = (f32[32,8,64]{2,1,0:T(8,128)S(1)}, f32[32,8,64]{2,1,0:T(8,128)S(1)}, u32[]{:S(2)}, u32[]{:S(2)}) collective-permute-start(f32[32,8,64]{2,1,0:T(8,128)S(1)} %copy.26), channel_id=1, source_target_pairs={{0,1},{1,2},{2,3},{3,4},{4,5},{5,6},{6,7},{7,0},{8,9},{9,10},{10,1... | collective-permute-start | bytes 196616 | tf_op jit(solution)/shard_map/ppermute | solution.py:11
  68.0 8.1 %copy-start.2 = (bf16[32,8,128]{2,1,0:T(8,128)(2,1)S(1)}, bf16[32,8,128]{2,1,0:T(8,128)(2,1)}, u32[]{:S(2)}) copy-start(bf16[32,8,128]{2,1,0:T(8,128)(2,1)} %param.15) | copy-start | bytes 196612
  68.3 13.0 %copy-start.1 = (s32[1,1,6144]{2,1,0:T(1,128)S(1)}, s32[1,1,6144]{2,1,0:T(1,128)}, u32[]{:S(2)}) copy-start(s32[1,1,6144]{2,1,0:T(1,128)} %param.17) | copy-start | bytes 73732
  76.2 8.1 %collective-permute-start.2 = (f32[32,8,64]{2,1,0:T(8,128)S(1)}, f32[32,8,64]{2,1,0:T(8,128)S(1)}, u32[]{:S(2)}, u32[]{:S(2)}) collective-permute-start(f32[32,8,64]{2,1,0:T(8,128)S(1)} %get-tuple-element.32), channel_id=1, source_target_pairs={{0,1},{1,2},{2,3},{3,4},{4,5},{5,6},{6,7},{7,0},{8,9},{9,10},{10,1... | collective-permute-start | bytes 196616 | tf_op jit(solution)/shard_map/ppermute | solution.py:21
  76.3 8.8 %collective-permute-start.3 = (f32[32,8,64]{2,1,0:T(8,128)S(1)}, f32[32,8,64]{2,1,0:T(8,128)S(1)}, u32[]{:S(2)}, u32[]{:S(2)}) collective-permute-start(f32[32,8,64]{2,1,0:T(8,128)S(1)} %get-tuple-element.33), channel_id=1, source_target_pairs={{1,0},{2,1},{3,2},{4,3},{5,4},{6,5},{7,6},{0,7},{9,8},{10,9},{11,1... | collective-permute-start | bytes 196616 | tf_op jit(solution)/shard_map/ppermute | solution.py:23
  137.0 0.7 copy-start.3
where the time goes:
time: 180 us; the launch traced here: 179 us
  other arithmetic  111 us (62%)
  blocking collectives  39.5 us (22%)
  starting transfers between devices  11.2 us (6%)
  local copies, waits for them, and re-layouts  7.08 us (4%)
  waiting for transfers between devices  6.27 us (3%)
  matrix products  2.32 us (1%)
    scatter-add x1, other arithmetic, spread(): return totals.at[:, pixel_ids].add(contribution)  56.4 us
    scatter-add x1, other arithmetic, gather_back(): return totals.at[:, cell_ids].add(contribution)  51 us
    psum x1, blocking collectives, per_device(): head_total, bias_total = lax.psum((head_part, bias_part), ('lat', 'lon'))  39.5 us
    ppermute x2, starting transfers between devices, from_behind(): lax.ppermute(shard, axis, [(i, (i + by) % devices) for i in range(devices)])  6.12 us
    ppermute x1, starting transfers between devices, with_halo(): lax.ppermute(head, axis, [((i + 1) % count, i) for i in range(count)])  4.96 us
    scatter-add x1, local copies, waits for them, and re-layouts, per_device(): own_tiles = own_part.at[:, :, tile_cols - rim_width:].add(from_east)  4.77 us
  transfers between devices with their start and end apart: 4, of which 4 were waited for; matrix products, arithmetic and copies ran while one was open for 3% of the time, Pallas kernels for 0%

commit v1 on v0

v1 whole, which is shorter than its diff:
```python
import functools
import math

import jax
import jax.numpy as jnp
from jax import lax
from jax.experimental import pallas as pl
from jax.experimental.pallas import tpu as pltpu
from jax.sharding import PartitionSpec as P

BF16 = jnp.bfloat16
F32 = jnp.float32
NN = (((1,), (0,)), ((), ()))
NT = (((1,), (1,)), ((), ()))
TN = (((0,), (0,)), ((), ()))


def dot(a, b, dims):
    return lax.dot_general(a, b, dims, preferred_element_type=F32)


def low_one_hot(ids, low):
    rows = lax.broadcasted_iota(jnp.int32, (low, ids.shape[1]), 0)
    return jnp.where(rows == (ids & (low - 1)), 1.0, 0.0).astype(BF16)


def pick_group(stacked, high, groups):
    size = stacked.shape[0] // groups
    picked = stacked[:size]
    for g in range(1, groups):
        picked = jnp.where(high == g, stacked[g * size : (g + 1) * size], picked)
    return picked


def spread_groups(values, high, groups):
    return jnp.concatenate(
        [jnp.where(high == g, values, 0.0).astype(BF16) for g in range(groups)], axis=0
    )


def live_weights(weight_ref, live, start, span):
    index = lax.broadcasted_iota(jnp.int32, (1, span), 1) + start
    return jnp.where(index < live, weight_ref[:, pl.ds(start, span)], 0.0)


def forward_kernel(
    span,
    live_ref,
    latent_ref,
    head_ref,
    bias_ref,
    targets_ref,
    cell_ref,
    pixel_ref,
    weight_ref,
    frame_ref,
    west_ref,
    east_ref,
    predicted,
    wide_targets,
):
    cycles, low_cells, _ = latent_ref.shape
    variables, tile_rows, tile_cols = targets_ref.shape
    frame_width = 2 * tile_cols
    rim = tile_cols // 2
    live = live_ref[0, 0]
    eye = lax.broadcasted_iota(jnp.int32, (variables, variables), 0) == lax.broadcasted_iota(
        jnp.int32, (variables, variables), 1
    )
    bias = jnp.sum(jnp.where(eye, bias_ref[...], 0.0), axis=1, keepdims=True)
    head_t = head_ref[...].astype(F32).T.astype(BF16)
    for c in range(cycles):
        predicted[c * variables : (c + 1) * variables, :] = (
            dot(head_t, latent_ref[c], NT) + bias
        ).astype(BF16)
    wide_targets[...] = targets_ref[...].astype(F32)
    frame_ref[...] = jnp.zeros_like(frame_ref)
    for start in range(0, cell_ref.shape[1], span):
        cell = cell_ref[:, pl.ds(start, span)]
        pixel = pixel_ref[:, pl.ds(start, span)]
        weight = live_weights(weight_ref, live, start, span)
        gathered = dot(predicted[...], low_one_hot(cell, low_cells), NN)
        share = pick_group(gathered, cell // low_cells, cycles) * weight
        frame_ref[...] += dot(
            spread_groups(share, pixel // frame_width, tile_rows),
            low_one_hot(pixel, frame_width),
            NT,
        )
    for t in range(tile_rows):
        rows = slice(t * variables, (t + 1) * variables)
        frame_ref[rows, rim : rim + tile_cols] -= wide_targets[:, t, :]
    west_ref[...] = frame_ref[:, :tile_cols].astype(BF16)
    east_ref[...] = frame_ref[:, tile_cols:].astype(BF16)


def backward_kernel(
    span,
    tile_rows,
    live_ref,
    frame_ref,
    from_west_ref,
    from_east_ref,
    latent_ref,
    head_ref,
    cell_ref,
    pixel_ref,
    weight_ref,
    latent_grad_ref,
    part_ref,
    misfit,
    totals,
):
    cycles, low_cells, _ = latent_ref.shape
    variables = head_ref.shape[1]
    frame_width = frame_ref.shape[1]
    half = frame_width // 2
    live = live_ref[0, 0]
    misfit[:, :half] = (frame_ref[:, :half] + from_west_ref[...].astype(F32)).astype(BF16)
    misfit[:, half:] = (frame_ref[:, half:] + from_east_ref[...].astype(F32)).astype(BF16)
    totals[...] = jnp.zeros_like(totals)
    for start in range(0, cell_ref.shape[1], span):
        cell = cell_ref[:, pl.ds(start, span)]
        pixel = pixel_ref[:, pl.ds(start, span)]
        weight = live_weights(weight_ref, live, start, span)
        gathered = dot(misfit[...], low_one_hot(pixel, frame_width), NN)
        share = pick_group(gathered, pixel // frame_width, tile_rows) * weight
        totals[...] += dot(
            spread_groups(share, cell // low_cells, cycles), low_one_hot(cell, low_cells), NT
        )
    head_t = head_ref[...].astype(F32).T.astype(BF16)
    head_part = jnp.zeros((variables, latent_ref.shape[2]), F32)
    bias_part = jnp.zeros((variables, 1), F32)
    for c in range(cycles):
        cell_misfit = totals[c * variables : (c + 1) * variables, :].astype(BF16)
        wide = cell_misfit.astype(F32)
        head_part += dot(cell_misfit, latent_ref[c], NN)
        bias_part += jnp.sum(wide, axis=1, keepdims=True)
        latent_grad_ref[c] = dot(wide.T.astype(BF16), head_t, NN).astype(BF16)
    part_ref[...] = jnp.zeros_like(part_ref)
    part_ref[:variables, :] = head_part
    eye = lax.broadcasted_iota(jnp.int32, (variables, variables), 0) == lax.broadcasted_iota(
        jnp.int32, (variables, variables), 1
    )
    part_ref[variables : variables + 1, :variables] = jnp.sum(
        jnp.where(eye, bias_part, 0.0), axis=0, keepdims=True
    )


def sum_over(value, axis):
    devices = lax.axis_size(axis)
    if devices & (devices - 1):
        return lax.psum(value, axis)
    step = 1
    while step < devices:
        value = value + lax.ppermute(value, axis, [(i, i ^ step) for i in range(devices)])
        step *= 2
    return value


def from_behind(shard, axis, by):
    devices = lax.axis_size(axis)
    return lax.ppermute(shard, axis, [(i, (i + by) % devices) for i in range(devices)])


def per_device(latent, head, bias, targets, margin_cell, margin_pixel, margin_weight, live_count):
    cycles, low_cells, width = latent.shape
    variables, tile_rows, tile_cols = targets.shape
    frame_shape = (tile_rows * variables, 2 * tile_cols)
    half_shape = (tile_rows * variables, tile_cols)
    cell_shape = (cycles * variables, low_cells)
    cell = margin_cell.reshape(1, -1)
    pixel = margin_pixel.reshape(1, -1)
    weight = margin_weight.reshape(1, -1)
    span = min(512, cell.shape[1])
    smem = pl.BlockSpec(memory_space=pltpu.SMEM)
    vmem = pl.BlockSpec(memory_space=pltpu.VMEM)
    params = pltpu.CompilerParams(vmem_limit_bytes=32 * 1024 * 1024)
    frame, west, east = pl.pallas_call(
        functools.partial(forward_kernel, span),
        out_shape=(
            jax.ShapeDtypeStruct(frame_shape, F32),
            jax.ShapeDtypeStruct(half_shape, BF16),
            jax.ShapeDtypeStruct(half_shape, BF16),
        ),
        in_specs=[smem] + [vmem] * 7,
        out_specs=(vmem, vmem, vmem),
        scratch_shapes=[
            pltpu.VMEM(cell_shape, BF16),
            pltpu.VMEM((variables, tile_rows, tile_cols), F32),
        ],
        compiler_params=params,
        name="forward",
    )(live_count, latent, head, bias.reshape(1, -1), targets, cell, pixel, weight)
    from_west = from_behind(east, "lon", 1)
    from_east = from_behind(west, "lon", -1)
    latent_grad, part = pl.pallas_call(
        functools.partial(backward_kernel, span, tile_rows),
        out_shape=(
            jax.ShapeDtypeStruct(latent.shape, BF16),
            jax.ShapeDtypeStruct((variables + 8, width), F32),
        ),
        in_specs=[smem] + [vmem] * 8,
        out_specs=(vmem, vmem),
        scratch_shapes=[
            pltpu.VMEM(frame_shape, BF16),
            pltpu.VMEM(cell_shape, F32),
        ],
        compiler_params=params,
        name="backward",
    )(live_count, frame, from_west, from_east, latent, head, cell, pixel, weight)
    total = sum_over(sum_over(part, "lat"), "lon")
    cell_total = cycles * low_cells * lax.axis_size("lat") * lax.axis_size("lon")
    total = total * (1.0 / math.sqrt(cell_total))
    return latent_grad, total[:variables].T, total[variables, :variables]


def solution(mesh):
    in_specs = (
        P("lat", "lon", None),
        P(),
        P(),
        P(None, "lat", "lon"),
        P("lat", "lon", None),
        P("lat", "lon", None),
        P("lat", "lon", None),
        P("lat", "lon"),
    )
    out_specs = (P("lat", "lon", None), P(), P())
    return jax.shard_map(
        per_device, mesh=mesh, in_specs=in_specs, out_specs=out_specs, check_vma=False
    )
```

time: 180 us -> 39.2 us (0.22)
  other arithmetic: 111 us -> 0.02 us
  blocking collectives: 39.5 us -> 0 us
  waiting for transfers between devices: 6.27 us -> 15.2 us
  Pallas kernels: 0 us -> 6.1 us
  matrix products: 2.32 us -> 0 us
  local copies, waits for them, and re-layouts: 7.08 us -> 5.2 us
    scatter-add x2 -> x0, other arithmetic: 107 us -> none  [the longest x1 56.4 us: spread(): return totals.at[:, pixel_ids].add(contribution)]
    psum x1 -> x0, blocking collectives: 39.5 us -> none  [per_device(): head_total, bias_total = lax.psum((head_part, bias_part), ('lat', 'lon'))]
    ppermute x2 -> x5, waiting for transfers between devices: 3.84 us -> 12.6 us  [sum_over(): lax.ppermute(value, axis, [(i, i ^ step) for i in range(devices)])]
    pallas_call x0 -> x2, Pallas kernels: none -> 6.1 us  [the longest x1 3.42 us: per_device(): pl.pallas_call(functools.partial(backward_kernel, span, tile_rows), out_s...]
    scatter-add x2 -> x0, local copies, waits for them, and re-layouts: 5.24 us -> none  [the longest x1 4.77 us: per_device(): own_tiles = own_part.at[:, :, tile_cols - rim_width:].add(from_east)]
    unnamed x14 -> x13, local copies, waits for them, and re-layouts: 1.02 us -> 4.08 us
    dot_general x3 -> x0, matrix products: 2.32 us -> none  [the longest x1 1.06 us: per_device(): lax.dot_general(cell_misfit, head, (((0,), (1,)), ((), ())), preferred_el...]
    ppermute x2 -> x5, starting transfers between devices: 5.12 us -> 4.84 us  [sum_over(): lax.ppermute(value, axis, [(i, i ^ step) for i in range(devices)])]
  transfers between devices with their start and end apart: 4 -> 7, of which waited for: 4 -> 7; matrix products, arithmetic and copies ran while one was open for 3% -> 0% of each run, Pallas kernels for 0% -> 0%
where the time goes in v1:
time: 39.2 us; the launch traced here: 38.8 us
  waiting for transfers between devices  15.2 us (39%)
  starting transfers between devices  11 us (28%)
  Pallas kernels  6.1 us (16%)
  local copies, waits for them, and re-layouts  5.2 us (13%)
  between operations  1.34 us (3%)
    ppermute x5, waiting for transfers between devices, sum_over(): lax.ppermute(value, axis, [(i, i ^ step) for i in range(devices)])  12.6 us
    ppermute x2, starting transfers between devices, from_behind(): lax.ppermute(shard, axis, [(i, (i + by) % devices) for i in range(devices)])  6.12 us
    ppermute x5, starting transfers between devices, sum_over(): lax.ppermute(value, axis, [(i, i ^ step) for i in range(devices)])  4.84 us
    unnamed x13, local copies, waits for them, and re-layouts  4.08 us
    pallas_call x1, Pallas kernels, per_device(): pl.pallas_call(functools.partial(backward_kernel, span, tile_rows), out_s...  3.42 us
    pallas_call x1, Pallas kernels, per_device(): pl.pallas_call(functools.partial(forward_kernel, span), out_shape=(jax.Sh...  2.68 us
    ppermute x2, waiting for transfers between devices, from_behind(): lax.ppermute(shard, axis, [(i, (i + by) % devices) for i in range(devices)])  2.57 us
  transfers between devices with their start and end apart: 7, of which 7 were waited for; matrix products, arithmetic and copies ran while one was open for 0% of the time, Pallas kernels for 0%

profile of v1, /device:TPU:0, one launch (start us, length us, event | category | flops | bytes accessed | tf_op | source)
XLA Modules:
  0.0 38.8 jit_solution(8008860515132491446)
XLA Ops:
  0.6 0.0 copy-start.2
  1.3 0.0 copy-start.1
  1.3 0.8 %copy.11.head_ref = bf16[128,32]{1,0:T(8,128)(2,1)S(1)} copy(bf16[128,32]{0,1:T(8,128)(2,1)} %param.9) | data formatting | bytes 16384 | tf_op args[1]
  2.1 0.0 copy-start.5
  2.1 0.0 copy-done.2
  2.1 0.0 copy-done.1
  2.1 0.6 %copy-done.5 = f32[32]{0:T(128)S(1)} copy-done((f32[32]{0:T(128)S(1)}, f32[32]{0:T(128)}, u32[]{:S(2)}) %copy-start.5) | copy-done | bytes 152
  2.8 0.0 copy-start
  2.8 1.0 %copy-done = bf16[8,256,128]{2,1,0:T(8,128)(2,1)S(1)} copy-done((bf16[8,256,128]{2,1,0:T(8,128)(2,1)S(1)}, bf16[8,256,128]{2,1,0:T(8,128)(2,1)}, u32[]{:S(2)}) %copy-start) | copy-done | bytes 524312
  3.8 0.0 copy-start.3
  3.8 0.7 %copy-done.3 = f32[1,1,6144]{2,1,0:T(1,128)S(1)} copy-done((f32[1,1,6144]{2,1,0:T(1,128)S(1)}, f32[1,1,6144]{2,1,0:T(1,128)}, u32[]{:S(2)}) %copy-start.3) | copy-done | bytes 24600
  4.6 0.0 copy-start.4
  4.6 0.8 %copy-done.4 = bf16[32,8,128]{2,1,0:T(8,128)(2,1)S(1)} copy-done((bf16[32,8,128]{2,1,0:T(8,128)(2,1)S(1)}, bf16[32,8,128]{2,1,0:T(8,128)(2,1)}, u32[]{:S(2)}) %copy-start.4) | copy-done | bytes 65560
  5.4 2.7 %forward.1 = (f32[256,256]{1,0:T(8,128)S(1)}, bf16[256,128]{1,0:T(8,128)(2,1)S(1)}, bf16[256,128]{1,0:T(8,128)(2,1)S(1)}) custom-call(s32[1,1]{1,0:T(1,128)S(6)} %copy.13.live_ref, bf16[8,256,128]{2,1,0:T(8,128)(2,1)S(1)} %copy-done, bf16[128,32]{1,0:T(8,128)(2,1)S(1)} %copy.11.head_ref, f32[1,32]{1,0:T(1,128)S(1)} %bitcast.14, ...), custom_call_target="tpu_custom_call" | custom-call | tf_op jit(solution)/shard_map/forward/pallas_call | solution.py:178
  8.1 3.0 %collective-permute-start = (bf16[256,128]{1,0:T(8,128)(2,1)S(1)}, bf16[256,128]{1,0:T(8,128)(2,1)S(1)}, u32[]{:S(2)}, u32[]{:S(2)}) collective-permute-start(bf16[256,128]{1,0:T(8,128)(2,1)S(1)} %get-tuple-element.9), channel_id=1, source_target_pairs={{0,1},{1,2},{2,3},{3,4},{4,5},{5,6},{6,7},{7,0},{8,9},{9,10},{10,1... | collective-permute-start | bytes 196616 | tf_op jit(solution)/shard_map/ppermute | solution.py:162
  11.1 3.1 %collective-permute-start.1 = (bf16[256,128]{1,0:T(8,128)(2,1)S(1)}, bf16[256,128]{1,0:T(8,128)(2,1)S(1)}, u32[]{:S(2)}, u32[]{:S(2)}) collective-permute-start(bf16[256,128]{1,0:T(8,128)(2,1)S(1)} %get-tuple-element.10), channel_id=1, source_target_pairs={{0,7},{1,0},{2,1},{3,2},{4,3},{5,4},{6,5},{7,6},{8,15},{9,8},{10,9... | collective-permute-start | bytes 196616 | tf_op jit(solution)/shard_map/ppermute | solution.py:162
  14.2 2.2 %collective-permute-done.from_west_ref = bf16[256,128]{1,0:T(8,128)(2,1)S(1)} collective-permute-done((bf16[256,128]{1,0:T(8,128)(2,1)S(1)}, bf16[256,128]{1,0:T(8,128)(2,1)S(1)}, u32[]{:S(2)}, u32[]{:S(2)}) %collective-permute-start) | collective-permute-done | bytes 65568 | tf_op jit(solution)/shard_map/ppermute | solution.py:162
  16.4 0.3 collective-permute-done.1.from_east_ref
  16.8 3.4 %backward.1 = (bf16[8,256,128]{2,1,0:T(8,128)(2,1)}, f32[40,128]{1,0:T(8,128)S(1)}) custom-call(s32[1,1]{1,0:T(1,128)S(6)} %copy.13.live_ref, f32[256,256]{1,0:T(8,128)S(1)} %get-tuple-element.8.frame_ref, bf16[256,128]{1,0:T(8,128)(2,1)S(1)} %collective-permute-done.from_west_ref, bf16[256,128]{1,0:T(8,128)(2,1)S(1)} %collective-permute-done.1.from_east_ref, ...), custom_call_target="tpu_custom_call" | custom-call | tf_op jit(solution)/shard_map/backward/pallas_call | solution.py:196
  20.2 0.0 collective-permute-start.2
  20.2 1.2 %collective-permute-done.2 = f32[40,128]{1,0:T(8,128)S(1)} collective-permute-done((f32[40,128]{1,0:T(8,128)S(1)}, f32[40,128]{1,0:T(8,128)S(1)}, u32[]{:S(2)}, u32[]{:S(2)}) %collective-permute-start.2) | collective-permute-done | bytes 20512 | tf_op jit(solution)/shard_map/ppermute | solution.py:155
  21.4 1.5 %collective-permute-start.3 = (f32[40,128]{1,0:T(8,128)S(1)}, f32[40,128]{1,0:T(8,128)S(1)}, u32[]{:S(2)}, u32[]{:S(2)}) collective-permute-start(f32[40,128]{1,0:T(8,128)S(1)} %add.15), channel_id=1, source_target_pairs={{0,16},{8,24},{16,0},{24,8},{1,17},{9,25},{17,1},{25,9},{2,18},{10... | collective-permute-start | bytes 61448 | tf_op jit(solution)/shard_map/ppermute | solution.py:155
  22.9 2.3 %collective-permute-done.3 = f32[40,128]{1,0:T(8,128)S(1)} collective-permute-done((f32[40,128]{1,0:T(8,128)S(1)}, f32[40,128]{1,0:T(8,128)S(1)}, u32[]{:S(2)}, u32[]{:S(2)}) %collective-permute-start.3) | collective-permute-done | bytes 20512 | tf_op jit(solution)/shard_map/ppermute | solution.py:155
  25.2 1.0 %collective-permute-start.4 = (f32[40,128]{1,0:T(8,128)S(1)}, f32[40,128]{1,0:T(8,128)S(1)}, u32[]{:S(2)}, u32[]{:S(2)}) collective-permute-start(f32[40,128]{1,0:T(8,128)S(1)} %add.16), channel_id=1, source_target_pairs={{0,1},{1,0},{2,3},{3,2},{4,5},{5,4},{6,7},{7,6},{8,9},{9,8},{10,11... | collective-permute-start | bytes 61448 | tf_op jit(solution)/shard_map/ppermute | solution.py:155
  26.2 2.8 %collective-permute-done.4 = f32[40,128]{1,0:T(8,128)S(1)} collective-permute-done((f32[40,128]{1,0:T(8,128)S(1)}, f32[40,128]{1,0:T(8,128)S(1)}, u32[]{:S(2)}, u32[]{:S(2)}) %collective-permute-start.4) | collective-permute-done | bytes 20512 | tf_op jit(solution)/shard_map/ppermute | solution.py:155
  29.0 0.6 %collective-permute-start.5 = (f32[40,128]{1,0:T(8,128)S(1)}, f32[40,128]{1,0:T(8,128)S(1)}, u32[]{:S(2)}, u32[]{:S(2)}) collective-permute-start(f32[40,128]{1,0:T(8,128)S(1)} %add.17), channel_id=1, source_target_pairs={{0,2},{1,3},{2,0},{3,1},{4,6},{5,7},{6,4},{7,5},{8,10},{9,11},{10,... | collective-permute-start | bytes 61448 | tf_op jit(solution)/shard_map/ppermute | solution.py:155
  29.5 3.2 %collective-permute-done.5 = f32[40,128]{1,0:T(8,128)S(1)} collective-permute-done((f32[40,128]{1,0:T(8,128)S(1)}, f32[40,128]{1,0:T(8,128)S(1)}, u32[]{:S(2)}, u32[]{:S(2)}) %collective-permute-start.5) | collective-permute-done | bytes 20512 | tf_op jit(solution)/shard_map/ppermute | solution.py:155
  32.8 1.8 %collective-permute-start.6 = (f32[40,128]{1,0:T(8,128)S(1)}, f32[40,128]{1,0:T(8,128)S(1)}, u32[]{:S(2)}, u32[]{:S(2)}) collective-permute-start(f32[40,128]{1,0:T(8,128)S(1)} %add.18), channel_id=1, source_target_pairs={{0,4},{1,5},{2,6},{3,7},{4,0},{5,1},{6,2},{7,3},{8,12},{9,13},{10,... | collective-permute-start | bytes 61448 | tf_op jit(solution)/shard_map/ppermute | solution.py:155
  34.5 3.1 %collective-permute-done.6 = f32[40,128]{1,0:T(8,128)S(1)} collective-permute-done((f32[40,128]{1,0:T(8,128)S(1)}, f32[40,128]{1,0:T(8,128)S(1)}, u32[]{:S(2)}, u32[]{:S(2)}) %collective-permute-start.6) | collective-permute-done | bytes 20512 | tf_op jit(solution)/shard_map/ppermute | solution.py:155
  37.7 0.5 %slice_bitcast_fusion.1 = f32[32]{0:T(128)} fusion(f32[40,128]{1,0:T(8,128)S(1)} %add_multiply_fusion), kind=kLoop, calls=%fused_computation.2 | loop fusion | bytes 256 | tf_op jit(solution)/shard_map/squeeze | solution.py:214
  38.2 0.6 %slice_bitcast_fusion = f32[128,32]{0,1:T(8,128)} fusion(f32[40,128]{1,0:T(8,128)S(1)} %add_multiply_fusion), kind=kLoop, calls=%fused_computation.1 | loop fusion | bytes 32768 | tf_op jit(solution)/shard_map/transpose | solution.py:214
  (5 shorter events, 0.0 us)
Async XLA Ops:
  0.6 1.5 %copy-start.2 = (s32[1,1,6144]{2,1,0:T(1,128)S(1)}, s32[1,1,6144]{2,1,0:T(1,128)}, u32[]{:S(2)}) copy-start(s32[1,1,6144]{2,1,0:T(1,128)} %param.13) | copy-start | bytes 73732
  1.3 0.8 %copy-start.1 = (s32[1,1,6144]{2,1,0:T(1,128)S(1)}, s32[1,1,6144]{2,1,0:T(1,128)}, u32[]{:S(2)}) copy-start(s32[1,1,6144]{2,1,0:T(1,128)} %param.12) | copy-start | bytes 73732
  2.1 0.7 %copy-start.5 = (f32[32]{0:T(128)S(1)}, f32[32]{0:T(128)}, u32[]{:S(2)}) copy-start(f32[32]{0:T(128)} %param.10) | copy-start | bytes 388
  2.8 1.0 %copy-start = (bf16[8,256,128]{2,1,0:T(8,128)(2,1)S(1)}, bf16[8,256,128]{2,1,0:T(8,128)(2,1)}, u32[]{:S(2)}) copy-start(bf16[8,256,128]{2,1,0:T(8,128)(2,1)} %latent_ref.3) | copy-start | bytes 1572868
  3.8 0.7 %copy-start.3 = (f32[1,1,6144]{2,1,0:T(1,128)S(1)}, f32[1,1,6144]{2,1,0:T(1,128)}, u32[]{:S(2)}) copy-start(f32[1,1,6144]{2,1,0:T(1,128)} %param.14) | copy-start | bytes 73732
  4.6 0.8 %copy-start.4 = (bf16[32,8,128]{2,1,0:T(8,128)(2,1)S(1)}, bf16[32,8,128]{2,1,0:T(8,128)(2,1)}, u32[]{:S(2)}) copy-start(bf16[32,8,128]{2,1,0:T(8,128)(2,1)} %targets_ref.1) | copy-start | bytes 196612
  8.1 8.4 %collective-permute-start = (bf16[256,128]{1,0:T(8,128)(2,1)S(1)}, bf16[256,128]{1,0:T(8,128)(2,1)S(1)}, u32[]{:S(2)}, u32[]{:S(2)}) collective-permute-start(bf16[256,128]{1,0:T(8,128)(2,1)S(1)} %get-tuple-element.9), channel_id=1, source_target_pairs={{0,1},{1,2},{2,3},{3,4},{4,5},{5,6},{6,7},{7,0},{8,9},{9,10},{10,1... | collective-permute-start | bytes 196616 | tf_op jit(solution)/shard_map/ppermute | solution.py:162
  11.1 5.7 %collective-permute-start.1 = (bf16[256,128]{1,0:T(8,128)(2,1)S(1)}, bf16[256,128]{1,0:T(8,128)(2,1)S(1)}, u32[]{:S(2)}, u32[]{:S(2)}) collective-permute-start(bf16[256,128]{1,0:T(8,128)(2,1)S(1)} %get-tuple-element.10), channel_id=1, source_target_pairs={{0,7},{1,0},{2,1},{3,2},{4,3},{5,4},{6,5},{7,6},{8,15},{9,8},{10,9... | collective-permute-start | bytes 196616 | tf_op jit(solution)/shard_map/ppermute | solution.py:162
  20.2 1.2 %collective-permute-start.2 = (f32[40,128]{1,0:T(8,128)S(1)}, f32[40,128]{1,0:T(8,128)S(1)}, u32[]{:S(2)}, u32[]{:S(2)}) collective-permute-start(f32[40,128]{1,0:T(8,128)S(1)} %get-tuple-element.12), channel_id=1, source_target_pairs={{0,8},{8,0},{16,24},{24,16},{1,9},{9,1},{17,25},{25,17},{2,10},{10... | collective-permute-start | bytes 61448 | tf_op jit(solution)/shard_map/ppermute | solution.py:155
  21.4 3.8 %collective-permute-start.3 = (f32[40,128]{1,0:T(8,128)S(1)}, f32[40,128]{1,0:T(8,128)S(1)}, u32[]{:S(2)}, u32[]{:S(2)}) collective-permute-start(f32[40,128]{1,0:T(8,128)S(1)} %add.15), channel_id=1, source_target_pairs={{0,16},{8,24},{16,0},{24,8},{1,17},{9,25},{17,1},{25,9},{2,18},{10... | collective-permute-start | bytes 61448 | tf_op jit(solution)/shard_map/ppermute | solution.py:155
  25.2 3.8 %collective-permute-start.4 = (f32[40,128]{1,0:T(8,128)S(1)}, f32[40,128]{1,0:T(8,128)S(1)}, u32[]{:S(2)}, u32[]{:S(2)}) collective-permute-start(f32[40,128]{1,0:T(8,128)S(1)} %add.16), channel_id=1, source_target_pairs={{0,1},{1,0},{2,3},{3,2},{4,5},{5,4},{6,7},{7,6},{8,9},{9,8},{10,11... | collective-permute-start | bytes 61448 | tf_op jit(solution)/shard_map/ppermute | solution.py:155
  29.0 3.8 %collective-permute-start.5 = (f32[40,128]{1,0:T(8,128)S(1)}, f32[40,128]{1,0:T(8,128)S(1)}, u32[]{:S(2)}, u32[]{:S(2)}) collective-permute-start(f32[40,128]{1,0:T(8,128)S(1)} %add.17), channel_id=1, source_target_pairs={{0,2},{1,3},{2,0},{3,1},{4,6},{5,7},{6,4},{7,5},{8,10},{9,11},{10,... | collective-permute-start | bytes 61448 | tf_op jit(solution)/shard_map/ppermute | solution.py:155
  32.8 4.9 %collective-permute-start.6 = (f32[40,128]{1,0:T(8,128)S(1)}, f32[40,128]{1,0:T(8,128)S(1)}, u32[]{:S(2)}, u32[]{:S(2)}) collective-permute-start(f32[40,128]{1,0:T(8,128)S(1)} %add.18), channel_id=1, source_target_pairs={{0,4},{1,5},{2,6},{3,7},{4,0},{5,1},{6,2},{7,3},{8,12},{9,13},{10,... | collective-permute-start | bytes 61448 | tf_op jit(solution)/shard_map/ppermute | solution.py:155

commit v2 on v1

v2 whole, which is shorter than its diff:
```python
import functools
import math

import jax
import jax.numpy as jnp
from jax import lax
from jax.experimental import pallas as pl
from jax.experimental.pallas import tpu as pltpu
from jax.sharding import PartitionSpec as P

BF16 = jnp.bfloat16
F32 = jnp.float32
NN = (((1,), (0,)), ((), ()))
NT = (((1,), (1,)), ((), ()))


def dot(a, b, dims):
    return lax.dot_general(a, b, dims, preferred_element_type=F32)


def low_one_hot(ids, low):
    rows = lax.broadcasted_iota(jnp.int32, (low, ids.shape[1]), 0)
    return jnp.where(rows == (ids & (low - 1)), 1.0, 0.0).astype(BF16)


def pick_group(stacked, high, groups):
    size = stacked.shape[0] // groups
    picked = stacked[:size]
    for g in range(1, groups):
        picked = jnp.where(high == g, stacked[g * size : (g + 1) * size], picked)
    return picked


def spread_groups(values, high, groups):
    return jnp.concatenate(
        [jnp.where(high == g, values, 0.0).astype(BF16) for g in range(groups)], axis=0
    )


def eye(size):
    rows = lax.broadcasted_iota(jnp.int32, (size, size), 0)
    return rows == lax.broadcasted_iota(jnp.int32, (size, size), 1)


def forward_kernel(
    span,
    live_ref,
    latent_hbm,
    head_hbm,
    bias_hbm,
    targets_hbm,
    cell_hbm,
    pixel_hbm,
    weight_hbm,
    frame_ref,
    west_ref,
    east_ref,
    latent_ref,
    head_ref,
    cell_ref,
    pixel_ref,
    weight_ref,
    bias_ref,
    targets_ref,
    predicted,
    wide_targets,
    sems,
):
    copies = [
        pltpu.make_async_copy(source, target, sems.at[i])
        for i, (source, target) in enumerate(
            (
                (head_hbm, head_ref),
                (bias_hbm, bias_ref),
                (latent_hbm, latent_ref),
                (cell_hbm, cell_ref),
                (pixel_hbm, pixel_ref),
                (weight_hbm, weight_ref),
                (targets_hbm, targets_ref),
            )
        )
    ]
    for copy in copies:
        copy.start()
    cycles, low_cells, _ = latent_ref.shape
    variables, tile_rows, tile_cols = targets_ref.shape
    frame_width = 2 * tile_cols
    rim = tile_cols // 2
    frame_ref[...] = jnp.zeros_like(frame_ref)
    for copy in copies[:3]:
        copy.wait()
    bias = jnp.sum(jnp.where(eye(variables), bias_ref[...], 0.0), axis=1, keepdims=True)
    for c in range(cycles):
        predicted[c * variables : (c + 1) * variables, :] = (
            dot(head_ref[...], latent_ref[c], NT) + bias
        ).astype(BF16)
    for copy in copies[3:]:
        copy.wait()
    rows = lax.broadcasted_iota(jnp.int32, weight_ref.shape, 1)
    weight_ref[...] = jnp.where(rows < live_ref[0, 0], weight_ref[...], 0.0)
    wide_targets[...] = targets_ref[...].astype(F32)
    for start in range(0, cell_ref.shape[1], span):
        cell = cell_ref[:, pl.ds(start, span)]
        pixel = pixel_ref[:, pl.ds(start, span)]
        weight = weight_ref[:, pl.ds(start, span)]
        gathered = dot(predicted[...], low_one_hot(cell, low_cells), NN)
        share = pick_group(gathered, cell // low_cells, cycles) * weight
        frame_ref[...] += dot(
            spread_groups(share, pixel // frame_width, tile_rows),
            low_one_hot(pixel, frame_width),
            NT,
        )
    for t in range(tile_rows):
        rows = slice(t * variables, (t + 1) * variables)
        frame_ref[rows, rim : rim + tile_cols] -= wide_targets[:, t, :]
    west_ref[...] = frame_ref[:, :tile_cols].astype(BF16)
    east_ref[...] = frame_ref[:, tile_cols:].astype(BF16)


def backward_kernel(
    span,
    tile_rows,
    frame_ref,
    from_west_ref,
    from_east_ref,
    latent_ref,
    cell_ref,
    pixel_ref,
    weight_ref,
    cell_misfit_ref,
    part_ref,
    misfit,
    totals,
):
    cycles, low_cells, _ = latent_ref.shape
    frame_rows, frame_width = frame_ref.shape
    variables = frame_rows // tile_rows
    half = frame_width // 2
    misfit[:, :half] = (frame_ref[:, :half] + from_west_ref[...].astype(F32)).astype(BF16)
    misfit[:, half:] = (frame_ref[:, half:] + from_east_ref[...].astype(F32)).astype(BF16)
    totals[...] = jnp.zeros_like(totals)
    for start in range(0, cell_ref.shape[1], span):
        cell = cell_ref[:, pl.ds(start, span)]
        pixel = pixel_ref[:, pl.ds(start, span)]
        weight = weight_ref[:, pl.ds(start, span)]
        gathered = dot(misfit[...], low_one_hot(pixel, frame_width), NN)
        share = pick_group(gathered, pixel // frame_width, tile_rows) * weight
        totals[...] += dot(
            spread_groups(share, cell // low_cells, cycles), low_one_hot(cell, low_cells), NT
        )
    head_part = jnp.zeros((variables, latent_ref.shape[2]), F32)
    bias_part = jnp.zeros((variables, 1), F32)
    for c in range(cycles):
        rows = slice(c * variables, (c + 1) * variables)
        cell_misfit = totals[rows, :].astype(BF16)
        cell_misfit_ref[rows, :] = cell_misfit
        head_part += dot(cell_misfit, latent_ref[c], NN)
        bias_part += jnp.sum(cell_misfit.astype(F32), axis=1, keepdims=True)
    part_ref[...] = jnp.zeros_like(part_ref)
    part_ref[:variables, :] = head_part
    part_ref[variables : variables + 1, :variables] = jnp.sum(
        jnp.where(eye(variables), bias_part, 0.0), axis=0, keepdims=True
    )


def latent_kernel(cell_misfit_ref, head_ref, latent_grad_ref):
    variables = head_ref.shape[0]
    for c in range(latent_grad_ref.shape[0]):
        rows = slice(c * variables, (c + 1) * variables)
        wide = cell_misfit_ref[rows, :].astype(F32)
        latent_grad_ref[c] = dot(wide.T.astype(BF16), head_ref[...], NN).astype(BF16)


def finish_kernel(scale, mine_ref, theirs_ref, head_grad_ref, bias_grad_ref):
    variables = head_grad_ref.shape[0]
    head_grad_ref[...] = (mine_ref[:variables, :] + theirs_ref[:variables, :]) * scale
    last = slice(variables, variables + 1)
    bias_grad_ref[...] = (mine_ref[last, :variables] + theirs_ref[last, :variables]) * scale


def sum_rounds(lat, lon):
    rounds = []
    for size, make in ((lat, lambda s: (s, 0)), (lon, lambda s: (1 if lat > 1 else 0, s))):
        steps = [1 << k for k in range(size.bit_length() - 1)]
        while steps:
            pair, steps = steps[:2], steps[2:]
            rounds.append([make(s) for s in pair + ([pair[0] ^ pair[1]] if len(pair) > 1 else [])])
    return rounds


def add_pairs(values):
    while len(values) > 1:
        values = [values[i] + values[i + 1] for i in range(0, len(values), 2)]
    return values[0]


def sum_but_last(value):
    lat, lon = lax.axis_size("lat"), lax.axis_size("lon")

    def swap(shard, flip):
        pairs = [
            (i * lon + j, (i ^ flip[0]) * lon + (j ^ flip[1])) for i in range(lat) for j in range(lon)
        ]
        return lax.ppermute(shard, ("lat", "lon"), pairs)

    if lat & (lat - 1) or lon & (lon - 1) or lat * lon == 1:
        return lax.psum(value, ("lat", "lon")), jnp.zeros_like(value)
    rounds = sum_rounds(lat, lon)
    for flips in rounds[:-1]:
        value = add_pairs([value] + [swap(value, flip) for flip in flips])
    last = [value] + [swap(value, flip) for flip in rounds[-1]]
    return add_pairs(last[: len(last) // 2]), add_pairs(last[len(last) // 2 :])


def from_behind(shard, axis, by):
    devices = lax.axis_size(axis)
    return lax.ppermute(shard, axis, [(i, (i + by) % devices) for i in range(devices)])


def per_device(latent, head, bias, targets, margin_cell, margin_pixel, margin_weight, live_count):
    cycles, low_cells, width = latent.shape
    variables, tile_rows, tile_cols = targets.shape
    frame_shape = (tile_rows * variables, 2 * tile_cols)
    half_shape = (tile_rows * variables, tile_cols)
    cell_shape = (cycles * variables, low_cells)
    cell = margin_cell.reshape(1, -1)
    pixel = margin_pixel.reshape(1, -1)
    weight = margin_weight.reshape(1, -1)
    span = min(512, cell.shape[1])
    hbm = pl.BlockSpec(memory_space=pltpu.HBM)
    vmem = pl.BlockSpec(memory_space=pltpu.VMEM)
    params = pltpu.CompilerParams(vmem_limit_bytes=24 * 1024 * 1024)
    frame, west, east, latent, head_t, cell, pixel, weight = pl.pallas_call(
        functools.partial(forward_kernel, span),
        out_shape=(
            jax.ShapeDtypeStruct(frame_shape, F32),
            jax.ShapeDtypeStruct(half_shape, BF16),
            jax.ShapeDtypeStruct(half_shape, BF16),
            jax.ShapeDtypeStruct(latent.shape, BF16),
            jax.ShapeDtypeStruct((variables, width), BF16),
            jax.ShapeDtypeStruct(cell.shape, jnp.int32),
            jax.ShapeDtypeStruct(cell.shape, jnp.int32),
            jax.ShapeDtypeStruct(cell.shape, F32),
        ),
        in_specs=[pl.BlockSpec(memory_space=pltpu.SMEM)] + [hbm] * 7,
        out_specs=[vmem] * 8,
        scratch_shapes=[
            pltpu.VMEM((1, variables), F32),
            pltpu.VMEM(targets.shape, BF16),
            pltpu.VMEM(cell_shape, BF16),
            pltpu.VMEM((variables, tile_rows, tile_cols), F32),
            pltpu.SemaphoreType.DMA((7,)),
        ],
        compiler_params=params,
        name="forward",
    )(
        live_count,
        *(
            pltpu.with_memory_space_constraint(array, pltpu.HBM)
            for array in (latent, head.T, bias.reshape(1, -1), targets, cell, pixel, weight)
        ),
    )
    from_west = from_behind(east, "lon", 1)
    from_east = from_behind(west, "lon", -1)
    cell_misfit, part = pl.pallas_call(
        functools.partial(backward_kernel, span, tile_rows),
        out_shape=(
            jax.ShapeDtypeStruct(cell_shape, BF16),
            jax.ShapeDtypeStruct((variables + 8, width), F32),
        ),
        in_specs=[vmem] * 7,
        out_specs=(vmem, vmem),
        scratch_shapes=[
            pltpu.VMEM(frame_shape, BF16),
            pltpu.VMEM(cell_shape, F32),
        ],
        compiler_params=params,
        name="backward",
    )(frame, from_west, from_east, latent, cell, pixel, weight)
    latent_grad = pl.pallas_call(
        latent_kernel,
        out_shape=jax.ShapeDtypeStruct(latent.shape, BF16),
        in_specs=[vmem, vmem],
        out_specs=vmem,
        compiler_params=params,
        cost_estimate=pl.CostEstimate(
            flops=2 * cycles * low_cells * width * variables,
            bytes_accessed=2 * cycles * low_cells * width,
            transcendentals=0,
        ),
        name="latent_gradient",
    )(cell_misfit, head_t)
    mine, theirs = sum_but_last(part)
    cell_total = cycles * low_cells * lax.axis_size("lat") * lax.axis_size("lon")
    head_grad, bias_grad = pl.pallas_call(
        functools.partial(finish_kernel, 1.0 / math.sqrt(cell_total)),
        out_shape=(
            jax.ShapeDtypeStruct((variables, width), F32),
            jax.ShapeDtypeStruct((1, variables), F32),
        ),
        in_specs=[vmem, vmem],
        out_specs=(vmem, vmem),
        name="finish",
    )(mine, theirs)
    return latent_grad, head_grad.T, bias_grad.reshape(variables)


def solution(mesh):
    in_specs = (
        P("lat", "lon", None),
        P(),
        P(),
        P(None, "lat", "lon"),
        P("lat", "lon", None),
        P("lat", "lon", None),
        P("lat", "lon", None),
        P("lat", "lon"),
    )
    out_specs = (P("lat", "lon", None), P(), P())
    return jax.shard_map(
        per_device, mesh=mesh, in_specs=in_specs, out_specs=out_specs, check_vma=False
    )
```

time: 39.2 us -> 32 us (0.82)
  waiting for transfers between devices: 15.2 us -> 7.22 us
  local copies, waits for them, and re-layouts: 5.2 us -> 0.6 us
  starting transfers between devices: 11 us -> 13.9 us
  Pallas kernels: 6.1 us -> 8.76 us
    ppermute x5 -> x7, waiting for transfers between devices: 12.6 us -> 4.65 us  [swap(): return lax.ppermute(shard, ('lat', 'lon'), pairs)]
    unnamed x13 -> x4, local copies, waits for them, and re-layouts: 4.08 us -> 0.6 us
    ppermute x5 -> x7, starting transfers between devices: 4.84 us -> 7.78 us  [swap(): return lax.ppermute(shard, ('lat', 'lon'), pairs)]
    pallas_call x0 -> x2, Pallas kernels: none -> 2.52 us  [the longest x1 1.36 us: per_device(): pl.pallas_call(functools.partial(finish_kernel, 1.0 / math.sqrt(cell_tota...]
    pallas_call x1, Pallas kernels: 2.68 us -> 3.9 us  [per_device(): pl.pallas_call(functools.partial(forward_kernel, span), out_shape=(jax.Sh...]
    pallas_call x1, Pallas kernels: 3.42 us -> 2.34 us  [per_device(): pl.pallas_call(functools.partial(backward_kernel, span, tile_rows), out_s...]
    transpose x1 -> x0, local copies, waits for them, and re-layouts: 0.61 us -> none  [per_device(): return (latent_grad, total[:variables].T, total[variables, :variables])]
    squeeze x1 -> x0, local copies, waits for them, and re-layouts: 0.51 us -> none  [per_device(): return (latent_grad, total[:variables].T, total[variables, :variables])]
  transfers between devices with their start and end apart: 7 -> 9, of which waited for: 7 -> 8; matrix products, arithmetic and copies ran while one was open for 0% -> 0% of each run, Pallas kernels for 0% -> 4%
where the time goes in v2:
time: 32 us; the launch traced here: 31.8 us
  starting transfers between devices  13.9 us (43%)
  Pallas kernels  8.76 us (27%)
  waiting for transfers between devices  7.22 us (23%)
  between operations  1.32 us (4%)
  local copies, waits for them, and re-layouts  0.6 us (2%)
    ppermute x7, starting transfers between devices, swap(): return lax.ppermute(shard, ('lat', 'lon'), pairs)  7.78 us
    ppermute x2, starting transfers between devices, from_behind(): lax.ppermute(shard, axis, [(i, (i + by) % devices) for i in range(devices)])  6.12 us
    ppermute x7, waiting for transfers between devices, swap(): return lax.ppermute(shard, ('lat', 'lon'), pairs)  4.65 us
    pallas_call x1, Pallas kernels, per_device(): pl.pallas_call(functools.partial(forward_kernel, span), out_shape=(jax.Sh...  3.9 us
    ppermute x2, waiting for transfers between devices, from_behind(): lax.ppermute(shard, axis, [(i, (i + by) % devices) for i in range(devices)])  2.57 us
    pallas_call x1, Pallas kernels, per_device(): pl.pallas_call(functools.partial(backward_kernel, span, tile_rows), out_s...  2.34 us
    pallas_call x1, Pallas kernels, per_device(): pl.pallas_call(functools.partial(finish_kernel, 1.0 / math.sqrt(cell_tota...  1.36 us
    pallas_call x1, Pallas kernels, per_device(): pl.pallas_call(latent_kernel, out_shape=jax.ShapeDtypeStruct(latent.shape...  1.17 us
  transfers between devices with their start and end apart: 9, of which 8 were waited for; matrix products, arithmetic and copies ran while one was open for 0% of the time, Pallas kernels for 4%

profile of v2, /device:TPU:0, one launch (start us, length us, event | category | flops | bytes accessed | tf_op | source)
XLA Modules:
  0.0 31.8 jit_solution(9683637198823230045)
XLA Ops:
  1.3 3.9 %forward.1 = (f32[256,256]{1,0:T(8,128)S(1)}, bf16[256,128]{1,0:T(8,128)(2,1)S(1)}, bf16[256,128]{1,0:T(8,128)(2,1)S(1)}, bf16[8,256,128]{2,1,0:T(8,128)(2,1)S(1...) custom-call(s32[1,1]{1,0:T(1,128)S(6)} %copy.11.live_ref, ...), custom_call_target="tpu_custom_call" | custom-call | tf_op jit(solution)/shard_map/forward/pallas_call | solution.py:233
  5.2 3.0 %collective-permute-start = (bf16[256,128]{1,0:T(8,128)(2,1)S(1)}, bf16[256,128]{1,0:T(8,128)(2,1)S(1)}, u32[]{:S(2)}, u32[]{:S(2)}) collective-permute-start(bf16[256,128]{1,0:T(8,128)(2,1)S(1)} %get-tuple-element.16), channel_id=1, source_target_pairs={{0,1},{1,2},{2,3},{3,4},{4,5},{5,6},{6,7},{7,0},{8,9},{9,10},{10,1... | collective-permute-start | bytes 196616 | tf_op jit(solution)/shard_map/ppermute | solution.py:217
  8.2 3.1 %collective-permute-start.1 = (bf16[256,128]{1,0:T(8,128)(2,1)S(1)}, bf16[256,128]{1,0:T(8,128)(2,1)S(1)}, u32[]{:S(2)}, u32[]{:S(2)}) collective-permute-start(bf16[256,128]{1,0:T(8,128)(2,1)S(1)} %get-tuple-element.17), channel_id=1, source_target_pairs={{0,7},{1,0},{2,1},{3,2},{4,3},{5,4},{6,5},{7,6},{8,15},{9,8},{10,9... | collective-permute-start | bytes 196616 | tf_op jit(solution)/shard_map/ppermute | solution.py:217
  11.3 2.2 %collective-permute-done.from_west_ref = bf16[256,128]{1,0:T(8,128)(2,1)S(1)} collective-permute-done((bf16[256,128]{1,0:T(8,128)(2,1)S(1)}, bf16[256,128]{1,0:T(8,128)(2,1)S(1)}, u32[]{:S(2)}, u32[]{:S(2)}) %collective-permute-start) | collective-permute-done | bytes 65568 | tf_op jit(solution)/shard_map/ppermute | solution.py:217
  13.5 0.3 %collective-permute-done.1.from_east_ref = bf16[256,128]{1,0:T(8,128)(2,1)S(1)} collective-permute-done((bf16[256,128]{1,0:T(8,128)(2,1)S(1)}, bf16[256,128]{1,0:T(8,128)(2,1)S(1)}, u32[]{:S(2)}, u32[]{:S(2)}) %collective-permute-start.1) | collective-permute-done | bytes 65568 | tf_op jit(solution)/shard_map/ppermute | solution.py:217
  13.9 2.3 %backward.1 = (bf16[256,256]{1,0:T(8,128)(2,1)S(1)}, f32[40,128]{1,0:T(8,128)S(1)}) custom-call(f32[256,256]{1,0:T(8,128)S(1)} %get-tuple-element.15.frame_ref, bf16[256,128]{1,0:T(8,128)(2,1)S(1)} %collective-permute-done.from_west_ref, bf16[256,128]{1,0:T(8,128)(2,1)S(1)} %collective-permute-done.1.from_east_ref, ...), custom_call_target="tpu_custom_call" | custom-call | tf_op jit(solution)/shard_map/backward/pallas_call | solution.py:265
  16.2 0.1 collective-permute-start.4
  16.3 1.6 %collective-permute-start.3 = (f32[40,128]{1,0:T(8,128)S(1)}, f32[40,128]{1,0:T(8,128)S(1)}, u32[]{:S(2)}, u32[]{:S(2)}) collective-permute-start(f32[40,128]{1,0:T(8,128)S(1)} %get-tuple-element.24), channel_id=1, source_target_pairs={{0,16},{1,17},{2,18},{3,19},{4,20},{5,21},{6,22},{7,23},{8,24},{9,... | collective-permute-start | bytes 61448 | tf_op jit(solution)/shard_map/ppermute | solution.py:204
  17.9 0.3 collective-permute-start.2
  18.1 1.5 %collective-permute-done.4 = f32[40,128]{1,0:T(8,128)S(1)} collective-permute-done((f32[40,128]{1,0:T(8,128)S(1)}, f32[40,128]{1,0:T(8,128)S(1)}, u32[]{:S(2)}, u32[]{:S(2)}) %collective-permute-start.4) | collective-permute-done | bytes 20512 | tf_op jit(solution)/shard_map/ppermute | solution.py:204
  19.7 0.5 %collective-permute-done.3 = f32[40,128]{1,0:T(8,128)S(1)} collective-permute-done((f32[40,128]{1,0:T(8,128)S(1)}, f32[40,128]{1,0:T(8,128)S(1)}, u32[]{:S(2)}, u32[]{:S(2)}) %collective-permute-start.3) | collective-permute-done | bytes 20512 | tf_op jit(solution)/shard_map/ppermute | solution.py:204
  20.1 0.0 collective-permute-done.2
  20.2 2.1 %collective-permute-start.7 = (f32[40,128]{1,0:T(8,128)S(1)}, f32[40,128]{1,0:T(8,128)S(1)}, u32[]{:S(2)}, u32[]{:S(2)}) collective-permute-start(f32[40,128]{1,0:T(8,128)S(1)} %add_add_fusion.1), channel_id=1, source_target_pairs={{0,11},{1,10},{2,9},{3,8},{4,15},{5,14},{6,13},{7,12},{8,3},{9,2},... | collective-permute-start | bytes 61448 | tf_op jit(solution)/shard_map/ppermute | solution.py:204
  22.2 0.2 collective-permute-start.6
  22.4 1.0 %collective-permute-start.5 = (f32[40,128]{1,0:T(8,128)S(1)}, f32[40,128]{1,0:T(8,128)S(1)}, u32[]{:S(2)}, u32[]{:S(2)}) collective-permute-start(f32[40,128]{1,0:T(8,128)S(1)} %add_add_fusion.1), channel_id=1, source_target_pairs={{0,9},{1,8},{2,11},{3,10},{4,13},{5,12},{6,15},{7,14},{8,1},{9,0},... | collective-permute-start | bytes 61448 | tf_op jit(solution)/shard_map/ppermute | solution.py:204
  23.4 0.9 %collective-permute-done.7 = f32[40,128]{1,0:T(8,128)S(1)} collective-permute-done((f32[40,128]{1,0:T(8,128)S(1)}, f32[40,128]{1,0:T(8,128)S(1)}, u32[]{:S(2)}, u32[]{:S(2)}) %collective-permute-start.7) | collective-permute-done | bytes 20512 | tf_op jit(solution)/shard_map/ppermute | solution.py:204
  24.4 1.1 %collective-permute-done.6 = f32[40,128]{1,0:T(8,128)S(1)} collective-permute-done((f32[40,128]{1,0:T(8,128)S(1)}, f32[40,128]{1,0:T(8,128)S(1)}, u32[]{:S(2)}, u32[]{:S(2)}) %collective-permute-start.6) | collective-permute-done | bytes 20512 | tf_op jit(solution)/shard_map/ppermute | solution.py:204
  25.4 0.2 collective-permute-done.5
  25.7 0.0 copy-start
  25.7 2.6 %collective-permute-start.8 = (f32[40,128]{1,0:T(8,128)S(1)}, f32[40,128]{1,0:T(8,128)S(1)}, u32[]{:S(2)}, u32[]{:S(2)}) collective-permute-start(f32[40,128]{1,0:T(8,128)S(1)} %add_add_fusion.mine_ref), channel_id=1, source_target_pairs={{0,12},{1,13},{2,14},{3,15},{4,8},{5,9},{6,10},{7,11},{8,4},{9,5},... | collective-permute-start | bytes 61448 | tf_op jit(solution)/shard_map/ppermute | solution.py:204
  28.3 1.2 %latent_gradient.1 = bf16[8,256,128]{2,1,0:T(8,128)(2,1)} custom-call(bf16[256,256]{1,0:T(8,128)(2,1)S(1)} %get-tuple-element.22.cell_misfit_ref, bf16[32,128]{1,0:T(8,128)(2,1)S(1)} %get-tuple-element.23.head_ref), custom_call_target="tpu_custom_call" | custom-call | flops 16777216 | bytes 524288 | tf_op jit(solution)/shard_map/latent_gradient/pallas_call | solution.py:280
  29.5 0.0 copy-done
  29.5 0.4 %collective-permute-done.8.theirs_ref = f32[40,128]{1,0:T(8,128)S(1)} collective-permute-done((f32[40,128]{1,0:T(8,128)S(1)}, f32[40,128]{1,0:T(8,128)S(1)}, u32[]{:S(2)}, u32[]{:S(2)}) %collective-permute-start.8) | collective-permute-done | bytes 20512 | tf_op jit(solution)/shard_map/ppermute | solution.py:204
  29.9 0.0 copy-start.1
  29.9 0.6 %copy-done.1 = f32[40,128]{1,0:T(8,128)} copy-done((f32[40,128]{1,0:T(8,128)}, f32[40,128]{1,0:T(8,128)S(1)}, u32[]{:S(2)}) %copy-start.1) | copy-done | bytes 20504
  30.5 1.4 %finish.1 = (f32[32,128]{1,0:T(8,128)}, f32[1,32]{1,0:T(1,128)}) custom-call(f32[40,128]{1,0:T(8,128)} %copy-done, f32[40,128]{1,0:T(8,128)} %copy-done.1), custom_call_target="tpu_custom_call" | custom-call | tf_op jit(solution)/shard_map/finish/pallas_call | solution.py:295
  (2 shorter events, 0.0 us)
Async XLA Ops:
  5.2 8.4 %collective-permute-start = (bf16[256,128]{1,0:T(8,128)(2,1)S(1)}, bf16[256,128]{1,0:T(8,128)(2,1)S(1)}, u32[]{:S(2)}, u32[]{:S(2)}) collective-permute-start(bf16[256,128]{1,0:T(8,128)(2,1)S(1)} %get-tuple-element.16), channel_id=1, source_target_pairs={{0,1},{1,2},{2,3},{3,4},{4,5},{5,6},{6,7},{7,0},{8,9},{9,10},{10,1... | collective-permute-start | bytes 196616 | tf_op jit(solution)/shard_map/ppermute | solution.py:217
  8.2 5.7 %collective-permute-start.1 = (bf16[256,128]{1,0:T(8,128)(2,1)S(1)}, bf16[256,128]{1,0:T(8,128)(2,1)S(1)}, u32[]{:S(2)}, u32[]{:S(2)}) collective-permute-start(bf16[256,128]{1,0:T(8,128)(2,1)S(1)} %get-tuple-element.17), channel_id=1, source_target_pairs={{0,7},{1,0},{2,1},{3,2},{4,3},{5,4},{6,5},{7,6},{8,15},{9,8},{10,9... | collective-permute-start | bytes 196616 | tf_op jit(solution)/shard_map/ppermute | solution.py:217
  16.2 3.4 %collective-permute-start.4 = (f32[40,128]{1,0:T(8,128)S(1)}, f32[40,128]{1,0:T(8,128)S(1)}, u32[]{:S(2)}, u32[]{:S(2)}) collective-permute-start(f32[40,128]{1,0:T(8,128)S(1)} %get-tuple-element.24), channel_id=1, source_target_pairs={{0,24},{1,25},{2,26},{3,27},{4,28},{5,29},{6,30},{7,31},{8,16},{9,... | collective-permute-start | bytes 61448 | tf_op jit(solution)/shard_map/ppermute | solution.py:204
  16.3 3.8 %collective-permute-start.3 = (f32[40,128]{1,0:T(8,128)S(1)}, f32[40,128]{1,0:T(8,128)S(1)}, u32[]{:S(2)}, u32[]{:S(2)}) collective-permute-start(f32[40,128]{1,0:T(8,128)S(1)} %get-tuple-element.24), channel_id=1, source_target_pairs={{0,16},{1,17},{2,18},{3,19},{4,20},{5,21},{6,22},{7,23},{8,24},{9,... | collective-permute-start | bytes 61448 | tf_op jit(solution)/shard_map/ppermute | solution.py:204
  17.9 2.3 %collective-permute-start.2 = (f32[40,128]{1,0:T(8,128)S(1)}, f32[40,128]{1,0:T(8,128)S(1)}, u32[]{:S(2)}, u32[]{:S(2)}) collective-permute-start(f32[40,128]{1,0:T(8,128)S(1)} %get-tuple-element.24), channel_id=1, source_target_pairs={{0,8},{1,9},{2,10},{3,11},{4,12},{5,13},{6,14},{7,15},{8,0},{9,1},... | collective-permute-start | bytes 61448 | tf_op jit(solution)/shard_map/ppermute | solution.py:204
  20.2 4.2 %collective-permute-start.7 = (f32[40,128]{1,0:T(8,128)S(1)}, f32[40,128]{1,0:T(8,128)S(1)}, u32[]{:S(2)}, u32[]{:S(2)}) collective-permute-start(f32[40,128]{1,0:T(8,128)S(1)} %add_add_fusion.1), channel_id=1, source_target_pairs={{0,11},{1,10},{2,9},{3,8},{4,15},{5,14},{6,13},{7,12},{8,3},{9,2},... | collective-permute-start | bytes 61448 | tf_op jit(solution)/shard_map/ppermute | solution.py:204
  22.2 3.2 %collective-permute-start.6 = (f32[40,128]{1,0:T(8,128)S(1)}, f32[40,128]{1,0:T(8,128)S(1)}, u32[]{:S(2)}, u32[]{:S(2)}) collective-permute-start(f32[40,128]{1,0:T(8,128)S(1)} %add_add_fusion.1), channel_id=1, source_target_pairs={{0,10},{1,11},{2,8},{3,9},{4,14},{5,15},{6,12},{7,13},{8,2},{9,3},... | collective-permute-start | bytes 61448 | tf_op jit(solution)/shard_map/ppermute | solution.py:204
  22.4 3.2 %collective-permute-start.5 = (f32[40,128]{1,0:T(8,128)S(1)}, f32[40,128]{1,0:T(8,128)S(1)}, u32[]{:S(2)}, u32[]{:S(2)}) collective-permute-start(f32[40,128]{1,0:T(8,128)S(1)} %add_add_fusion.1), channel_id=1, source_target_pairs={{0,9},{1,8},{2,11},{3,10},{4,13},{5,12},{6,15},{7,14},{8,1},{9,0},... | collective-permute-start | bytes 61448 | tf_op jit(solution)/shard_map/ppermute | solution.py:204
  25.7 3.8 %copy-start = (f32[40,128]{1,0:T(8,128)}, f32[40,128]{1,0:T(8,128)S(1)}, u32[]{:S(2)}) copy-start(f32[40,128]{1,0:T(8,128)S(1)} %add_add_fusion.mine_ref) | copy-start | bytes 61444
  25.7 4.2 %collective-permute-start.8 = (f32[40,128]{1,0:T(8,128)S(1)}, f32[40,128]{1,0:T(8,128)S(1)}, u32[]{:S(2)}, u32[]{:S(2)}) collective-permute-start(f32[40,128]{1,0:T(8,128)S(1)} %add_add_fusion.mine_ref), channel_id=1, source_target_pairs={{0,12},{1,13},{2,14},{3,15},{4,8},{5,9},{6,10},{7,11},{8,4},{9,5},... | collective-permute-start | bytes 61448 | tf_op jit(solution)/shard_map/ppermute | solution.py:204
  29.9 0.6 %copy-start.1 = (f32[40,128]{1,0:T(8,128)}, f32[40,128]{1,0:T(8,128)S(1)}, u32[]{:S(2)}) copy-start(f32[40,128]{1,0:T(8,128)S(1)} %collective-permute-done.8.theirs_ref) | copy-start | bytes 61444

commit v3 on v2

--- a/solution.py
+++ b/solution.py
@@ -19,8 +19,8 @@
 
 
 def low_one_hot(ids, low):
-    rows = lax.broadcasted_iota(jnp.int32, (low, ids.shape[1]), 0)
-    return jnp.where(rows == (ids & (low - 1)), 1.0, 0.0).astype(BF16)
+    rows = lax.broadcasted_iota(jnp.int32, (low, ids.shape[1]), 0).astype(BF16)
+    return jnp.where(rows == (ids & (low - 1)).astype(BF16), jnp.ones((), BF16), jnp.zeros((), BF16))
 
 
 def pick_group(stacked, high, groups):
@@ -32,8 +32,9 @@
 
 
 def spread_groups(values, high, groups):
+    narrow = values.astype(BF16)
     return jnp.concatenate(
-        [jnp.where(high == g, values, 0.0).astype(BF16) for g in range(groups)], axis=0
+        [narrow * jnp.where(high == g, 1.0, 0.0).astype(BF16) for g in range(groups)], axis=0
     )
 
 
@@ -226,7 +227,7 @@
     cell = margin_cell.reshape(1, -1)
     pixel = margin_pixel.reshape(1, -1)
     weight = margin_weight.reshape(1, -1)
-    span = min(512, cell.shape[1])
+    span = min(1024, cell.shape[1])
     hbm = pl.BlockSpec(memory_space=pltpu.HBM)
     vmem = pl.BlockSpec(memory_space=pltpu.VMEM)
     params = pltpu.CompilerParams(vmem_limit_bytes=24 * 1024 * 1024)
@@ -300,6 +301,7 @@
         ),
         in_specs=[vmem, vmem],
         out_specs=(vmem, vmem),
+        compiler_params=pltpu.CompilerParams(vmem_limit_bytes=1024 * 1024),
         name="finish",
     )(mine, theirs)
     return latent_grad, head_grad.T, bias_grad.reshape(variables)

time: 32 us -> 30.1 us (0.941)
  Pallas kernels: 8.76 us -> 7.39 us
  local copies, waits for them, and re-layouts: 0.6 us -> 0 us
    pallas_call x1, Pallas kernels: 1.36 us -> 0.61 us  [per_device(): pl.pallas_call(functools.partial(finish_kernel, 1.0 / math.sqrt(cell_tota...]
    unnamed x4 -> x0, local copies, waits for them, and re-layouts: 0.6 us -> none
    pallas_call x1, Pallas kernels: 3.9 us -> 3.45 us  [per_device(): pl.pallas_call(functools.partial(forward_kernel, span), out_shape=(jax.Sh...]
where the time goes in v3:
time: 30.1 us; the launch traced here: 29.8 us
  starting transfers between devices  13.9 us (46%)
  Pallas kernels  7.39 us (25%)
  waiting for transfers between devices  7.2 us (24%)
  between operations  1.31 us (4%)
    ppermute x7, starting transfers between devices, swap(): return lax.ppermute(shard, ('lat', 'lon'), pairs)  7.79 us
    ppermute x2, starting transfers between devices, from_behind(): lax.ppermute(shard, axis, [(i, (i + by) % devices) for i in range(devices)])  6.12 us
    ppermute x7, waiting for transfers between devices, swap(): return lax.ppermute(shard, ('lat', 'lon'), pairs)  4.63 us
    pallas_call x1, Pallas kernels, per_device(): pl.pallas_call(functools.partial(forward_kernel, span), out_shape=(jax.Sh...  3.45 us
    ppermute x2, waiting for transfers between devices, from_behind(): lax.ppermute(shard, axis, [(i, (i + by) % devices) for i in range(devices)])  2.57 us
    pallas_call x1, Pallas kernels, per_device(): pl.pallas_call(functools.partial(backward_kernel, span, tile_rows), out_s...  2.15 us
    pallas_call x1, Pallas kernels, per_device(): pl.pallas_call(latent_kernel, out_shape=jax.ShapeDtypeStruct(latent.shape...  1.17 us
    pallas_call x1, Pallas kernels, per_device(): pl.pallas_call(functools.partial(finish_kernel, 1.0 / math.sqrt(cell_tota...  0.61 us
  transfers between devices with their start and end apart: 9, of which 8 were waited for; matrix products, arithmetic and copies ran while one was open for 0% of the time, Pallas kernels for 4%

profile of v3, /device:TPU:0, one launch (start us, length us, event | category | flops | bytes accessed | tf_op | source)
XLA Modules:
  0.0 29.8 jit_solution(11915703270037855980)
XLA Ops:
  1.3 3.5 %forward.1 = (f32[256,256]{1,0:T(8,128)S(1)}, bf16[256,128]{1,0:T(8,128)(2,1)S(1)}, bf16[256,128]{1,0:T(8,128)(2,1)S(1)}, bf16[8,256,128]{2,1,0:T(8,128)(2,1)S(1...) custom-call(s32[1,1]{1,0:T(1,128)S(6)} %copy.11.live_ref, ...), custom_call_target="tpu_custom_call" | custom-call | tf_op jit(solution)/shard_map/forward/pallas_call | solution.py:234
  4.7 3.0 %collective-permute-start = (bf16[256,128]{1,0:T(8,128)(2,1)S(1)}, bf16[256,128]{1,0:T(8,128)(2,1)S(1)}, u32[]{:S(2)}, u32[]{:S(2)}) collective-permute-start(bf16[256,128]{1,0:T(8,128)(2,1)S(1)} %get-tuple-element.16), channel_id=1, source_target_pairs={{0,1},{1,2},{2,3},{3,4},{4,5},{5,6},{6,7},{7,0},{8,9},{9,10},{10,1... | collective-permute-start | bytes 196616 | tf_op jit(solution)/shard_map/ppermute | solution.py:218
  7.8 3.1 %collective-permute-start.1 = (bf16[256,128]{1,0:T(8,128)(2,1)S(1)}, bf16[256,128]{1,0:T(8,128)(2,1)S(1)}, u32[]{:S(2)}, u32[]{:S(2)}) collective-permute-start(bf16[256,128]{1,0:T(8,128)(2,1)S(1)} %get-tuple-element.17), channel_id=1, source_target_pairs={{0,7},{1,0},{2,1},{3,2},{4,3},{5,4},{6,5},{7,6},{8,15},{9,8},{10,9... | collective-permute-start | bytes 196616 | tf_op jit(solution)/shard_map/ppermute | solution.py:218
  10.9 2.2 %collective-permute-done.from_west_ref = bf16[256,128]{1,0:T(8,128)(2,1)S(1)} collective-permute-done((bf16[256,128]{1,0:T(8,128)(2,1)S(1)}, bf16[256,128]{1,0:T(8,128)(2,1)S(1)}, u32[]{:S(2)}, u32[]{:S(2)}) %collective-permute-start) | collective-permute-done | bytes 65568 | tf_op jit(solution)/shard_map/ppermute | solution.py:218
  13.1 0.3 %collective-permute-done.1.from_east_ref = bf16[256,128]{1,0:T(8,128)(2,1)S(1)} collective-permute-done((bf16[256,128]{1,0:T(8,128)(2,1)S(1)}, bf16[256,128]{1,0:T(8,128)(2,1)S(1)}, u32[]{:S(2)}, u32[]{:S(2)}) %collective-permute-start.1) | collective-permute-done | bytes 65568 | tf_op jit(solution)/shard_map/ppermute | solution.py:218
  13.4 2.2 %backward.1 = (bf16[256,256]{1,0:T(8,128)(2,1)S(1)}, f32[40,128]{1,0:T(8,128)S(1)}) custom-call(f32[256,256]{1,0:T(8,128)S(1)} %get-tuple-element.15.frame_ref, bf16[256,128]{1,0:T(8,128)(2,1)S(1)} %collective-permute-done.from_west_ref, bf16[256,128]{1,0:T(8,128)(2,1)S(1)} %collective-permute-done.1.from_east_ref, ...), custom_call_target="tpu_custom_call" | custom-call | tf_op jit(solution)/shard_map/backward/pallas_call | solution.py:266
  15.6 0.1 collective-permute-start.4
  15.7 1.6 %collective-permute-start.3 = (f32[40,128]{1,0:T(8,128)S(1)}, f32[40,128]{1,0:T(8,128)S(1)}, u32[]{:S(2)}, u32[]{:S(2)}) collective-permute-start(f32[40,128]{1,0:T(8,128)S(1)} %get-tuple-element.24), channel_id=1, source_target_pairs={{0,16},{1,17},{2,18},{3,19},{4,20},{5,21},{6,22},{7,23},{8,24},{9,... | collective-permute-start | bytes 61448 | tf_op jit(solution)/shard_map/ppermute | solution.py:205
  17.2 0.3 collective-permute-start.2
  17.5 1.5 %collective-permute-done.4 = f32[40,128]{1,0:T(8,128)S(1)} collective-permute-done((f32[40,128]{1,0:T(8,128)S(1)}, f32[40,128]{1,0:T(8,128)S(1)}, u32[]{:S(2)}, u32[]{:S(2)}) %collective-permute-start.4) | collective-permute-done | bytes 20512 | tf_op jit(solution)/shard_map/ppermute | solution.py:205
  19.0 0.5 %collective-permute-done.3 = f32[40,128]{1,0:T(8,128)S(1)} collective-permute-done((f32[40,128]{1,0:T(8,128)S(1)}, f32[40,128]{1,0:T(8,128)S(1)}, u32[]{:S(2)}, u32[]{:S(2)}) %collective-permute-start.3) | collective-permute-done | bytes 20512 | tf_op jit(solution)/shard_map/ppermute | solution.py:205
  19.5 0.0 collective-permute-done.2
  19.5 2.1 %collective-permute-start.7 = (f32[40,128]{1,0:T(8,128)S(1)}, f32[40,128]{1,0:T(8,128)S(1)}, u32[]{:S(2)}, u32[]{:S(2)}) collective-permute-start(f32[40,128]{1,0:T(8,128)S(1)} %add_add_fusion.1), channel_id=1, source_target_pairs={{0,11},{1,10},{2,9},{3,8},{4,15},{5,14},{6,13},{7,12},{8,3},{9,2},... | collective-permute-start | bytes 61448 | tf_op jit(solution)/shard_map/ppermute | solution.py:205
  21.6 0.2 collective-permute-start.6
  21.8 1.0 %collective-permute-start.5 = (f32[40,128]{1,0:T(8,128)S(1)}, f32[40,128]{1,0:T(8,128)S(1)}, u32[]{:S(2)}, u32[]{:S(2)}) collective-permute-start(f32[40,128]{1,0:T(8,128)S(1)} %add_add_fusion.1), channel_id=1, source_target_pairs={{0,9},{1,8},{2,11},{3,10},{4,13},{5,12},{6,15},{7,14},{8,1},{9,0},... | collective-permute-start | bytes 61448 | tf_op jit(solution)/shard_map/ppermute | solution.py:205
  22.8 0.9 %collective-permute-done.7 = f32[40,128]{1,0:T(8,128)S(1)} collective-permute-done((f32[40,128]{1,0:T(8,128)S(1)}, f32[40,128]{1,0:T(8,128)S(1)}, u32[]{:S(2)}, u32[]{:S(2)}) %collective-permute-start.7) | collective-permute-done | bytes 20512 | tf_op jit(solution)/shard_map/ppermute | solution.py:205
  23.7 1.1 %collective-permute-done.6 = f32[40,128]{1,0:T(8,128)S(1)} collective-permute-done((f32[40,128]{1,0:T(8,128)S(1)}, f32[40,128]{1,0:T(8,128)S(1)}, u32[]{:S(2)}, u32[]{:S(2)}) %collective-permute-start.6) | collective-permute-done | bytes 20512 | tf_op jit(solution)/shard_map/ppermute | solution.py:205
  24.8 0.2 collective-permute-done.5
  25.0 2.6 %collective-permute-start.8 = (f32[40,128]{1,0:T(8,128)S(1)}, f32[40,128]{1,0:T(8,128)S(1)}, u32[]{:S(2)}, u32[]{:S(2)}) collective-permute-start(f32[40,128]{1,0:T(8,128)S(1)} %add_add_fusion.mine_ref), channel_id=1, source_target_pairs={{0,12},{1,13},{2,14},{3,15},{4,8},{5,9},{6,10},{7,11},{8,4},{9,5},... | collective-permute-start | bytes 61448 | tf_op jit(solution)/shard_map/ppermute | solution.py:205
  27.7 1.2 %latent_gradient.1 = bf16[8,256,128]{2,1,0:T(8,128)(2,1)} custom-call(bf16[256,256]{1,0:T(8,128)(2,1)S(1)} %get-tuple-element.22.cell_misfit_ref, bf16[32,128]{1,0:T(8,128)(2,1)S(1)} %get-tuple-element.23.head_ref), custom_call_target="tpu_custom_call" | custom-call | flops 16777216 | bytes 524288 | tf_op jit(solution)/shard_map/latent_gradient/pallas_call | solution.py:281
  28.8 0.4 %collective-permute-done.8.theirs_ref = f32[40,128]{1,0:T(8,128)S(1)} collective-permute-done((f32[40,128]{1,0:T(8,128)S(1)}, f32[40,128]{1,0:T(8,128)S(1)}, u32[]{:S(2)}, u32[]{:S(2)}) %collective-permute-start.8) | collective-permute-done | bytes 20512 | tf_op jit(solution)/shard_map/ppermute | solution.py:205
  29.2 0.6 %finish.1 = (f32[32,128]{1,0:T(8,128)}, f32[1,32]{1,0:T(1,128)}) custom-call(f32[40,128]{1,0:T(8,128)S(1)} %add_add_fusion.mine_ref, f32[40,128]{1,0:T(8,128)S(1)} %collective-permute-done.8.theirs_ref), custom_call_target="tpu_custom_call" | custom-call | tf_op jit(solution)/shard_map/finish/pallas_call | solution.py:296
  (2 shorter events, 0.0 us)
Async XLA Ops:
  4.7 8.4 %collective-permute-start = (bf16[256,128]{1,0:T(8,128)(2,1)S(1)}, bf16[256,128]{1,0:T(8,128)(2,1)S(1)}, u32[]{:S(2)}, u32[]{:S(2)}) collective-permute-start(bf16[256,128]{1,0:T(8,128)(2,1)S(1)} %get-tuple-element.16), channel_id=1, source_target_pairs={{0,1},{1,2},{2,3},{3,4},{4,5},{5,6},{6,7},{7,0},{8,9},{9,10},{10,1... | collective-permute-start | bytes 196616 | tf_op jit(solution)/shard_map/ppermute | solution.py:218
  7.8 5.7 %collective-permute-start.1 = (bf16[256,128]{1,0:T(8,128)(2,1)S(1)}, bf16[256,128]{1,0:T(8,128)(2,1)S(1)}, u32[]{:S(2)}, u32[]{:S(2)}) collective-permute-start(bf16[256,128]{1,0:T(8,128)(2,1)S(1)} %get-tuple-element.17), channel_id=1, source_target_pairs={{0,7},{1,0},{2,1},{3,2},{4,3},{5,4},{6,5},{7,6},{8,15},{9,8},{10,9... | collective-permute-start | bytes 196616 | tf_op jit(solution)/shard_map/ppermute | solution.py:218
  15.6 3.4 %collective-permute-start.4 = (f32[40,128]{1,0:T(8,128)S(1)}, f32[40,128]{1,0:T(8,128)S(1)}, u32[]{:S(2)}, u32[]{:S(2)}) collective-permute-start(f32[40,128]{1,0:T(8,128)S(1)} %get-tuple-element.24), channel_id=1, source_target_pairs={{0,24},{1,25},{2,26},{3,27},{4,28},{5,29},{6,30},{7,31},{8,16},{9,... | collective-permute-start | bytes 61448 | tf_op jit(solution)/shard_map/ppermute | solution.py:205
  15.7 3.8 %collective-permute-start.3 = (f32[40,128]{1,0:T(8,128)S(1)}, f32[40,128]{1,0:T(8,128)S(1)}, u32[]{:S(2)}, u32[]{:S(2)}) collective-permute-start(f32[40,128]{1,0:T(8,128)S(1)} %get-tuple-element.24), channel_id=1, source_target_pairs={{0,16},{1,17},{2,18},{3,19},{4,20},{5,21},{6,22},{7,23},{8,24},{9,... | collective-permute-start | bytes 61448 | tf_op jit(solution)/shard_map/ppermute | solution.py:205
  17.2 2.3 %collective-permute-start.2 = (f32[40,128]{1,0:T(8,128)S(1)}, f32[40,128]{1,0:T(8,128)S(1)}, u32[]{:S(2)}, u32[]{:S(2)}) collective-permute-start(f32[40,128]{1,0:T(8,128)S(1)} %get-tuple-element.24), channel_id=1, source_target_pairs={{0,8},{1,9},{2,10},{3,11},{4,12},{5,13},{6,14},{7,15},{8,0},{9,1},... | collective-permute-start | bytes 61448 | tf_op jit(solution)/shard_map/ppermute | solution.py:205
  19.5 4.2 %collective-permute-start.7 = (f32[40,128]{1,0:T(8,128)S(1)}, f32[40,128]{1,0:T(8,128)S(1)}, u32[]{:S(2)}, u32[]{:S(2)}) collective-permute-start(f32[40,128]{1,0:T(8,128)S(1)} %add_add_fusion.1), channel_id=1, source_target_pairs={{0,11},{1,10},{2,9},{3,8},{4,15},{5,14},{6,13},{7,12},{8,3},{9,2},... | collective-permute-start | bytes 61448 | tf_op jit(solution)/shard_map/ppermute | solution.py:205
  21.6 3.2 %collective-permute-start.6 = (f32[40,128]{1,0:T(8,128)S(1)}, f32[40,128]{1,0:T(8,128)S(1)}, u32[]{:S(2)}, u32[]{:S(2)}) collective-permute-start(f32[40,128]{1,0:T(8,128)S(1)} %add_add_fusion.1), channel_id=1, source_target_pairs={{0,10},{1,11},{2,8},{3,9},{4,14},{5,15},{6,12},{7,13},{8,2},{9,3},... | collective-permute-start | bytes 61448 | tf_op jit(solution)/shard_map/ppermute | solution.py:205
  21.8 3.2 %collective-permute-start.5 = (f32[40,128]{1,0:T(8,128)S(1)}, f32[40,128]{1,0:T(8,128)S(1)}, u32[]{:S(2)}, u32[]{:S(2)}) collective-permute-start(f32[40,128]{1,0:T(8,128)S(1)} %add_add_fusion.1), channel_id=1, source_target_pairs={{0,9},{1,8},{2,11},{3,10},{4,13},{5,12},{6,15},{7,14},{8,1},{9,0},... | collective-permute-start | bytes 61448 | tf_op jit(solution)/shard_map/ppermute | solution.py:205
  25.0 4.2 %collective-permute-start.8 = (f32[40,128]{1,0:T(8,128)S(1)}, f32[40,128]{1,0:T(8,128)S(1)}, u32[]{:S(2)}, u32[]{:S(2)}) collective-permute-start(f32[40,128]{1,0:T(8,128)S(1)} %add_add_fusion.mine_ref), channel_id=1, source_target_pairs={{0,12},{1,13},{2,14},{3,15},{4,8},{5,9},{6,10},{7,11},{8,4},{9,5},... | collective-permute-start | bytes 61448 | tf_op jit(solution)/shard_map/ppermute | solution.py:205

commit v4 on v3

--- a/solution.py
+++ b/solution.py
@@ -71,9 +71,9 @@
         pltpu.make_async_copy(source, target, sems.at[i])
         for i, (source, target) in enumerate(
             (
+                (latent_hbm, latent_ref),
                 (head_hbm, head_ref),
                 (bias_hbm, bias_ref),
-                (latent_hbm, latent_ref),
                 (cell_hbm, cell_ref),
                 (pixel_hbm, pixel_ref),
                 (weight_hbm, weight_ref),
@@ -88,18 +88,19 @@
     frame_width = 2 * tile_cols
     rim = tile_cols // 2
     frame_ref[...] = jnp.zeros_like(frame_ref)
-    for copy in copies[:3]:
+    for copy in copies[:]:
         copy.wait()
     bias = jnp.sum(jnp.where(eye(variables), bias_ref[...], 0.0), axis=1, keepdims=True)
     for c in range(cycles):
         predicted[c * variables : (c + 1) * variables, :] = (
             dot(head_ref[...], latent_ref[c], NT) + bias
         ).astype(BF16)
-    for copy in copies[3:]:
-        copy.wait()
     rows = lax.broadcasted_iota(jnp.int32, weight_ref.shape, 1)
     weight_ref[...] = jnp.where(rows < live_ref[0, 0], weight_ref[...], 0.0)
     wide_targets[...] = targets_ref[...].astype(F32)
+    for t in range(tile_rows):
+        rows = slice(t * variables, (t + 1) * variables)
+        frame_ref[rows, rim : rim + tile_cols] = -wide_targets[:, t, :]
     for start in range(0, cell_ref.shape[1], span):
         cell = cell_ref[:, pl.ds(start, span)]
         pixel = pixel_ref[:, pl.ds(start, span)]
@@ -111,11 +112,20 @@
             low_one_hot(pixel, frame_width),
             NT,
         )
-    for t in range(tile_rows):
-        rows = slice(t * variables, (t + 1) * variables)
-        frame_ref[rows, rim : rim + tile_cols] -= wide_targets[:, t, :]
     west_ref[...] = frame_ref[:, :tile_cols].astype(BF16)
     east_ref[...] = frame_ref[:, tile_cols:].astype(BF16)
+
+
+def gather_latent_kernel(span, latent_ref, cell_ref, gathered_ref, table):
+    cycles, low_cells, width = latent_ref.shape
+    for c in range(cycles):
+        table[c * width : (c + 1) * width, :] = latent_ref[c].astype(F32).T.astype(BF16)
+    for start in range(0, gathered_ref.shape[1], span):
+        cell = cell_ref[:, pl.ds(start, span)]
+        gathered = dot(table[...], low_one_hot(cell, low_cells), NN)
+        gathered_ref[:, pl.ds(start, span)] = pick_group(
+            gathered, cell // low_cells, cycles
+        ).astype(BF16)
 
 
 def backward_kernel(
@@ -128,40 +138,64 @@
     cell_ref,
     pixel_ref,
     weight_ref,
-    cell_misfit_ref,
+    row_latent_ref,
+    share_ref,
+    totals_ref,
     part_ref,
     misfit,
-    totals,
 ):
-    cycles, low_cells, _ = latent_ref.shape
+    cycles, low_cells, width = latent_ref.shape
+    early = row_latent_ref.shape[1]
     frame_rows, frame_width = frame_ref.shape
     variables = frame_rows // tile_rows
     half = frame_width // 2
     misfit[:, :half] = (frame_ref[:, :half] + from_west_ref[...].astype(F32)).astype(BF16)
     misfit[:, half:] = (frame_ref[:, half:] + from_east_ref[...].astype(F32)).astype(BF16)
-    totals[...] = jnp.zeros_like(totals)
-    for start in range(0, cell_ref.shape[1], span):
-        cell = cell_ref[:, pl.ds(start, span)]
+    head_part = jnp.zeros((variables, width), F32)
+    bias_part = jnp.zeros((variables, 128), F32)
+    totals_ref[...] = jnp.zeros_like(totals_ref)
+    for start in reversed(range(0, pixel_ref.shape[1], span)):
         pixel = pixel_ref[:, pl.ds(start, span)]
-        weight = weight_ref[:, pl.ds(start, span)]
         gathered = dot(misfit[...], low_one_hot(pixel, frame_width), NN)
-        share = pick_group(gathered, pixel // frame_width, tile_rows) * weight
-        totals[...] += dot(
-            spread_groups(share, cell // low_cells, cycles), low_one_hot(cell, low_cells), NT
+        share = (
+            pick_group(gathered, pixel // frame_width, tile_rows)
+            * weight_ref[:, pl.ds(start, span)]
         )
-    head_part = jnp.zeros((variables, latent_ref.shape[2]), F32)
-    bias_part = jnp.zeros((variables, 1), F32)
+        for lane in range(0, span, 128):
+            bias_part += share[:, lane : lane + 128]
+        if start < early:
+            narrow = share.astype(BF16)
+            share_ref[:, pl.ds(start, span)] = narrow
+        else:
+            cell = cell_ref[:, pl.ds(start, span)]
+            totals_ref[...] += dot(
+                spread_groups(share, cell // low_cells, cycles), low_one_hot(cell, low_cells), NT
+            )
     for c in range(cycles):
         rows = slice(c * variables, (c + 1) * variables)
-        cell_misfit = totals[rows, :].astype(BF16)
-        cell_misfit_ref[rows, :] = cell_misfit
-        head_part += dot(cell_misfit, latent_ref[c], NN)
-        bias_part += jnp.sum(cell_misfit.astype(F32), axis=1, keepdims=True)
+        head_part += dot(totals_ref[rows, :].astype(BF16), latent_ref[c], NN)
+    head_part += dot(share_ref[...], row_latent_ref[...], NT)
     part_ref[...] = jnp.zeros_like(part_ref)
     part_ref[:variables, :] = head_part
     part_ref[variables : variables + 1, :variables] = jnp.sum(
-        jnp.where(eye(variables), bias_part, 0.0), axis=0, keepdims=True
+        jnp.where(eye(variables), jnp.sum(bias_part, axis=1, keepdims=True), 0.0),
+        axis=0,
+        keepdims=True,
     )
+
+
+def cell_kernel(span, share_ref, cell_ref, late_ref, cell_misfit_ref, totals):
+    variables, early = share_ref.shape
+    groups, low_cells = totals.shape[0] // variables, totals.shape[1]
+    totals[...] = late_ref[...]
+    for start in range(0, early, span):
+        cell = cell_ref[:, pl.ds(start, span)]
+        totals[...] += dot(
+            spread_groups(share_ref[:, pl.ds(start, span)], cell // low_cells, groups),
+            low_one_hot(cell, low_cells),
+            NT,
+        )
+    cell_misfit_ref[...] = totals[...].astype(BF16)
 
 
 def latent_kernel(cell_misfit_ref, head_ref, latent_grad_ref):
@@ -181,11 +215,16 @@
 
 def sum_rounds(lat, lon):
     rounds = []
-    for size, make in ((lat, lambda s: (s, 0)), (lon, lambda s: (1 if lat > 1 else 0, s))):
-        steps = [1 << k for k in range(size.bit_length() - 1)]
-        while steps:
-            pair, steps = steps[:2], steps[2:]
-            rounds.append([make(s) for s in pair + ([pair[0] ^ pair[1]] if len(pair) > 1 else [])])
+    low_first = [1 << k for k in range(lat.bit_length() - 1)]
+    while low_first:
+        pair, low_first = low_first[:2], low_first[2:]
+        rounds.append([(s, 0) for s in pair + [pair[0] ^ pair[-1]] * (len(pair) - 1)])
+    cross = min(lat - 1, 1)
+    high_first = [1 << k for k in reversed(range(lon.bit_length() - 1))]
+    while high_first:
+        take = 2 - len(high_first) % 2
+        pair, high_first = high_first[:take], high_first[take:]
+        rounds.append([(cross, s) for s in pair + [pair[0] ^ pair[-1]] * (take - 1)])
     return rounds
 
 
@@ -195,7 +234,7 @@
     return values[0]
 
 
-def sum_but_last(value):
+def sum_but_last(value, jobs):
     lat, lon = lax.axis_size("lat"), lax.axis_size("lon")
 
     def swap(shard, flip):
@@ -204,13 +243,23 @@
         ]
         return lax.ppermute(shard, ("lat", "lon"), pairs)
 
-    if lat & (lat - 1) or lon & (lon - 1) or lat * lon == 1:
-        return lax.psum(value, ("lat", "lon")), jnp.zeros_like(value)
-    rounds = sum_rounds(lat, lon)
+    jobs, done = list(jobs), None
+    powers = lat & (lat - 1) == 0 and lon & (lon - 1) == 0
+    rounds = sum_rounds(lat, lon) if powers else []
     for flips in rounds[:-1]:
-        value = add_pairs([value] + [swap(value, flip) for flip in flips])
+        shards = [value] + [swap(value, flip) for flip in flips]
+        if jobs:
+            done = jobs.pop(0)(done)
+            value, done = lax.optimization_barrier((add_pairs(shards), done))
+        else:
+            value = add_pairs(shards)
+    for job in jobs:
+        done = job(done)
+    if not rounds:
+        return lax.psum(value, ("lat", "lon")), jnp.zeros_like(value), done
     last = [value] + [swap(value, flip) for flip in rounds[-1]]
-    return add_pairs(last[: len(last) // 2]), add_pairs(last[len(last) // 2 :])
+    half = len(last) // 2
+    return add_pairs(last[:half]), add_pairs(last[half:]), done
 
 
 def from_behind(shard, axis, by):
@@ -227,7 +276,7 @@
     cell = margin_cell.reshape(1, -1)
     pixel = margin_pixel.reshape(1, -1)
     weight = margin_weight.reshape(1, -1)
-    span = min(1024, cell.shape[1])
+    span = math.gcd(1024, cell.shape[1])
     hbm = pl.BlockSpec(memory_space=pltpu.HBM)
     vmem = pl.BlockSpec(memory_space=pltpu.VMEM)
     params = pltpu.CompilerParams(vmem_limit_bytes=24 * 1024 * 1024)
@@ -263,35 +312,68 @@
     )
     from_west = from_behind(east, "lon", 1)
     from_east = from_behind(west, "lon", -1)
-    cell_misfit, part = pl.pallas_call(
+    row_total = cell.shape[1]
+    early = row_total * 2 // 3 // span * span
+    row_latent = pl.pallas_call(
+        functools.partial(gather_latent_kernel, span),
+        out_shape=jax.ShapeDtypeStruct((width, early), BF16),
+        in_specs=[vmem, vmem],
+        out_specs=vmem,
+        scratch_shapes=[pltpu.VMEM((cycles * width, low_cells), BF16)],
+        compiler_params=params,
+        cost_estimate=pl.CostEstimate(
+            flops=2 * cycles * width * low_cells * early,
+            bytes_accessed=2 * width * early,
+            transcendentals=0,
+        ),
+        name="gather_latent",
+    )(latent, cell)
+    share, totals, part = pl.pallas_call(
         functools.partial(backward_kernel, span, tile_rows),
         out_shape=(
-            jax.ShapeDtypeStruct(cell_shape, BF16),
+            jax.ShapeDtypeStruct((variables, early), BF16),
+            jax.ShapeDtypeStruct(cell_shape, F32),
             jax.ShapeDtypeStruct((variables + 8, width), F32),
         ),
-        in_specs=[vmem] * 7,
-        out_specs=(vmem, vmem),
-        scratch_shapes=[
-            pltpu.VMEM(frame_shape, BF16),
-            pltpu.VMEM(cell_shape, F32),
-        ],
+        in_specs=[vmem] * 8,
+        out_specs=(vmem, vmem, vmem),
+        scratch_shapes=[pltpu.VMEM(frame_shape, BF16)],
         compiler_params=params,
         name="backward",
-    )(frame, from_west, from_east, latent, cell, pixel, weight)
-    latent_grad = pl.pallas_call(
-        latent_kernel,
-        out_shape=jax.ShapeDtypeStruct(latent.shape, BF16),
-        in_specs=[vmem, vmem],
-        out_specs=vmem,
-        compiler_params=params,
-        cost_estimate=pl.CostEstimate(
-            flops=2 * cycles * low_cells * width * variables,
-            bytes_accessed=2 * cycles * low_cells * width,
-            transcendentals=0,
-        ),
-        name="latent_gradient",
-    )(cell_misfit, head_t)
-    mine, theirs = sum_but_last(part)
+    )(frame, from_west, from_east, latent, cell, pixel, weight, row_latent)
+
+    def add_early_cells(_):
+        return pl.pallas_call(
+            functools.partial(cell_kernel, span),
+            out_shape=jax.ShapeDtypeStruct(cell_shape, BF16),
+            in_specs=[vmem] * 3,
+            out_specs=vmem,
+            scratch_shapes=[pltpu.VMEM(cell_shape, F32)],
+            compiler_params=params,
+            cost_estimate=pl.CostEstimate(
+                flops=2 * cycles * variables * low_cells * row_total,
+                bytes_accessed=2 * variables * row_total,
+                transcendentals=0,
+            ),
+            name="cells",
+        )(share, cell, totals)
+
+    def grad_of_latent(cell_misfit):
+        return pl.pallas_call(
+            latent_kernel,
+            out_shape=jax.ShapeDtypeStruct(latent.shape, BF16),
+            in_specs=[vmem, vmem],
+            out_specs=vmem,
+            compiler_params=params,
+            cost_estimate=pl.CostEstimate(
+                flops=2 * cycles * low_cells * width * variables,
+                bytes_accessed=2 * cycles * low_cells * width,
+                transcendentals=0,
+            ),
+            name="latent_gradient",
+        )(cell_misfit, head_t)
+
+    mine, theirs, latent_grad = sum_but_last(part, (add_early_cells, grad_of_latent))
     cell_total = cycles * low_cells * lax.axis_size("lat") * lax.axis_size("lon")
     head_grad, bias_grad = pl.pallas_call(
         functools.partial(finish_kernel, 1.0 / math.sqrt(cell_total)),

time: 30.1 us -> 29.4 us (0.977)
  Pallas kernels: 7.39 us -> 10.1 us
  waiting for transfers between devices: 7.2 us -> 5.05 us
  starting transfers between devices: 13.9 us -> 12.8 us
    pallas_call x1 -> x3, Pallas kernels: 1.17 us -> 4.38 us  [the longest x1 2.45 us: per_device(): pl.pallas_call(functools.partial(gather_latent_kernel, span), out_shape=j...]
    ppermute x2, waiting for transfers between devices: 2.57 us -> 0.1 us  [from_behind(): lax.ppermute(shard, axis, [(i, (i + by) % devices) for i in range(devices)])]
    ppermute x7, starting transfers between devices: 7.79 us -> 6.65 us  [swap(): return lax.ppermute(shard, ('lat', 'lon'), pairs)]
    pallas_call x1, Pallas kernels: 2.15 us -> 1.66 us  [per_device(): pl.pallas_call(functools.partial(backward_kernel, span, tile_rows), out_s...]
    ppermute x7, waiting for transfers between devices: 4.63 us -> 4.95 us  [swap(): return lax.ppermute(shard, ('lat', 'lon'), pairs)]
  transfers between devices with their start and end apart: 9 -> 9, of which waited for: 8 -> 6; matrix products, arithmetic and copies ran while one was open for 0% -> 0% of each run, Pallas kernels for 4% -> 15%
where the time goes in v4:
time: 29.4 us; the launch traced here: 29.2 us
  starting transfers between devices  12.8 us (44%)
  Pallas kernels  10.1 us (34%)
  waiting for transfers between devices  5.05 us (17%)
  between operations  1.33 us (5%)
    ppermute x7, starting transfers between devices, swap(): return lax.ppermute(shard, ('lat', 'lon'), pairs)  6.65 us
    ppermute x2, starting transfers between devices, from_behind(): lax.ppermute(shard, axis, [(i, (i + by) % devices) for i in range(devices)])  6.12 us
    ppermute x7, waiting for transfers between devices, swap(): return lax.ppermute(shard, ('lat', 'lon'), pairs)  4.95 us
    pallas_call x1, Pallas kernels, per_device(): pl.pallas_call(functools.partial(forward_kernel, span), out_shape=(jax.Sh...  3.4 us
    pallas_call x1, Pallas kernels, per_device(): pl.pallas_call(functools.partial(gather_latent_kernel, span), out_shape=j...  2.45 us
    pallas_call x1, Pallas kernels, per_device(): pl.pallas_call(functools.partial(backward_kernel, span, tile_rows), out_s...  1.66 us
    pallas_call x1, Pallas kernels, grad_of_latent(): pl.pallas_call(latent_kernel, out_shape=jax.ShapeDtypeStruct(latent.shape...  1.17 us
    pallas_call x1, Pallas kernels, add_early_cells(): pl.pallas_call(functools.partial(cell_kernel, span), out_shape=jax.ShapeD...  0.76 us
  transfers between devices with their start and end apart: 9, of which 6 were waited for; matrix products, arithmetic and copies ran while one was open for 0% of the time, Pallas kernels for 15%

profile of v4, /device:TPU:0, one launch (start us, length us, event | category | flops | bytes accessed | tf_op | source)
XLA Modules:
  0.0 29.2 jit_solution(17072327197082431857)
XLA Ops:
  1.3 3.4 %forward.1 = (f32[256,256]{1,0:T(8,128)S(1)}, bf16[256,128]{1,0:T(8,128)(2,1)S(1)}, bf16[256,128]{1,0:T(8,128)(2,1)S(1)}, bf16[8,256,128]{2,1,0:T(8,128)(2,1)S(1...) custom-call(s32[1,1]{1,0:T(1,128)S(6)} %copy.11.live_ref, ...), custom_call_target="tpu_custom_call" | custom-call | tf_op jit(solution)/shard_map/forward/pallas_call | solution.py:283
  4.7 3.0 %collective-permute-start = (bf16[256,128]{1,0:T(8,128)(2,1)S(1)}, bf16[256,128]{1,0:T(8,128)(2,1)S(1)}, u32[]{:S(2)}, u32[]{:S(2)}) collective-permute-start(bf16[256,128]{1,0:T(8,128)(2,1)S(1)} %get-tuple-element.21), channel_id=1, source_target_pairs={{0,1},{1,2},{2,3},{3,4},{4,5},{5,6},{6,7},{7,0},{8,9},{9,10},{10,1... | collective-permute-start | bytes 196616 | tf_op jit(solution)/shard_map/ppermute | solution.py:267
  7.7 3.1 %collective-permute-start.1 = (bf16[256,128]{1,0:T(8,128)(2,1)S(1)}, bf16[256,128]{1,0:T(8,128)(2,1)S(1)}, u32[]{:S(2)}, u32[]{:S(2)}) collective-permute-start(bf16[256,128]{1,0:T(8,128)(2,1)S(1)} %get-tuple-element.22), channel_id=1, source_target_pairs={{0,7},{1,0},{2,1},{3,2},{4,3},{5,4},{6,5},{7,6},{8,15},{9,8},{10,9... | collective-permute-start | bytes 196616 | tf_op jit(solution)/shard_map/ppermute | solution.py:267
  10.8 2.5 %gather_latent.1.row_latent_ref = bf16[128,4096]{1,0:T(8,128)(2,1)S(1)} custom-call(bf16[8,256,128]{2,1,0:T(8,128)(2,1)S(1)} %get-tuple-element.23.latent_ref, s32[1,6144]{1,0:T(1,128)S(1)} %get-tuple-element.24.cell_ref), custom_call_target="tpu_custom_call" | custom-call | flops 2147483648 | bytes 1048576 | tf_op jit(solution)/shard_map/gather_latent/pallas_call | solution.py:317
  13.3 0.0 collective-permute-done.from_west_ref
  13.3 0.1 collective-permute-done.1.from_east_ref
  13.4 1.7 %backward.1 = (bf16[32,4096]{1,0:T(8,128)(2,1)S(1)}, f32[256,256]{1,0:T(8,128)S(1)}, f32[40,128]{1,0:T(8,128)S(1)}) custom-call(f32[256,256]{1,0:T(8,128)S(1)} %get-tuple-element.20.frame_ref, bf16[256,128]{1,0:T(8,128)(2,1)S(1)} %collective-permute-done.from_west_ref, bf16[256,128]{1,0:T(8,128)(2,1)S(1)} %collective-permute-done.1.from_east_ref, ...), custom_call_target="tpu_custom_call" | custom-call | tf_op jit(solution)/shard_map/backward/pallas_call | solution.py:331
  15.0 0.6 %collective-permute-start.4 = (f32[40,128]{1,0:T(8,128)S(1)}, f32[40,128]{1,0:T(8,128)S(1)}, u32[]{:S(2)}, u32[]{:S(2)}) collective-permute-start(f32[40,128]{1,0:T(8,128)S(1)} %get-tuple-element.27), channel_id=1, source_target_pairs={{0,24},{1,25},{2,26},{3,27},{4,28},{5,29},{6,30},{7,31},{8,16},{9,... | collective-permute-start | bytes 61448 | tf_op jit(solution)/shard_map/ppermute | solution.py:244
  15.7 1.0 %collective-permute-start.3 = (f32[40,128]{1,0:T(8,128)S(1)}, f32[40,128]{1,0:T(8,128)S(1)}, u32[]{:S(2)}, u32[]{:S(2)}) collective-permute-start(f32[40,128]{1,0:T(8,128)S(1)} %get-tuple-element.27), channel_id=1, source_target_pairs={{0,16},{1,17},{2,18},{3,19},{4,20},{5,21},{6,22},{7,23},{8,24},{9,... | collective-permute-start | bytes 61448 | tf_op jit(solution)/shard_map/ppermute | solution.py:244
  16.7 0.3 collective-permute-start.2
  17.0 0.8 %cells.1.cell_misfit_ref = bf16[256,256]{1,0:T(8,128)(2,1)S(1)} custom-call(bf16[32,4096]{1,0:T(8,128)(2,1)S(1)} %get-tuple-element.28.share_ref, s32[1,6144]{1,0:T(1,128)S(1)} %get-tuple-element.24.cell_ref, f32[256,256]{1,0:T(8,128)S(1)} %get-tuple-element.29.late_ref), custom_call_target="tpu_custom_call" | custom-call | flops 805306368 | bytes 393216 | tf_op jit(solution)/shard_map/cells/pallas_call | solution.py:346
  17.7 0.7 %collective-permute-done.4 = f32[40,128]{1,0:T(8,128)S(1)} collective-permute-done((f32[40,128]{1,0:T(8,128)S(1)}, f32[40,128]{1,0:T(8,128)S(1)}, u32[]{:S(2)}, u32[]{:S(2)}) %collective-permute-start.4) | collective-permute-done | bytes 20512 | tf_op jit(solution)/shard_map/ppermute | solution.py:244
  18.5 1.1 %collective-permute-done.3 = f32[40,128]{1,0:T(8,128)S(1)} collective-permute-done((f32[40,128]{1,0:T(8,128)S(1)}, f32[40,128]{1,0:T(8,128)S(1)}, u32[]{:S(2)}, u32[]{:S(2)}) %collective-permute-start.3) | collective-permute-done | bytes 20512 | tf_op jit(solution)/shard_map/ppermute | solution.py:244
  19.6 0.0 collective-permute-done.2
  19.6 1.4 %collective-permute-start.5 = (f32[40,128]{1,0:T(8,128)S(1)}, f32[40,128]{1,0:T(8,128)S(1)}, u32[]{:S(2)}, u32[]{:S(2)}) collective-permute-start(f32[40,128]{1,0:T(8,128)S(1)} %add_add_fusion), channel_id=1, source_target_pairs={{0,12},{1,13},{2,14},{3,15},{4,8},{5,9},{6,10},{7,11},{8,4},{9,5},... | collective-permute-start | bytes 61448 | tf_op jit(solution)/shard_map/ppermute | solution.py:244
  21.0 1.2 %latent_gradient.1 = bf16[8,256,128]{2,1,0:T(8,128)(2,1)} custom-call(bf16[256,256]{1,0:T(8,128)(2,1)S(1)} %cells.1.cell_misfit_ref, bf16[32,128]{1,0:T(8,128)(2,1)S(1)} %get-tuple-element.32.head_ref), custom_call_target="tpu_custom_call" | custom-call | flops 16777216 | bytes 524288 | tf_op jit(solution)/shard_map/latent_gradient/pallas_call | solution.py:362
  22.2 1.6 %collective-permute-done.5 = f32[40,128]{1,0:T(8,128)S(1)} collective-permute-done((f32[40,128]{1,0:T(8,128)S(1)}, f32[40,128]{1,0:T(8,128)S(1)}, u32[]{:S(2)}, u32[]{:S(2)}) %collective-permute-start.5) | collective-permute-done | bytes 20512 | tf_op jit(solution)/shard_map/ppermute | solution.py:244
  23.8 0.4 %collective-permute-start.6 = (f32[40,128]{1,0:T(8,128)S(1)}, f32[40,128]{1,0:T(8,128)S(1)}, u32[]{:S(2)}, u32[]{:S(2)}) collective-permute-start(f32[40,128]{1,0:T(8,128)S(1)} %add.21), channel_id=1, source_target_pairs={{0,10},{1,11},{2,8},{3,9},{4,14},{5,15},{6,12},{7,13},{8,2},{9,3},... | collective-permute-start | bytes 61448 | tf_op jit(solution)/shard_map/ppermute | solution.py:244
  24.2 1.2 %collective-permute-start.8 = (f32[40,128]{1,0:T(8,128)S(1)}, f32[40,128]{1,0:T(8,128)S(1)}, u32[]{:S(2)}, u32[]{:S(2)}) collective-permute-start(f32[40,128]{1,0:T(8,128)S(1)} %add.21), channel_id=1, source_target_pairs={{0,11},{1,10},{2,9},{3,8},{4,15},{5,14},{6,13},{7,12},{8,3},{9,2},... | collective-permute-start | bytes 61448 | tf_op jit(solution)/shard_map/ppermute | solution.py:244
  25.4 1.7 %collective-permute-start.7 = (f32[40,128]{1,0:T(8,128)S(1)}, f32[40,128]{1,0:T(8,128)S(1)}, u32[]{:S(2)}, u32[]{:S(2)}) collective-permute-start(f32[40,128]{1,0:T(8,128)S(1)} %add.21), channel_id=1, source_target_pairs={{0,9},{1,8},{2,11},{3,10},{4,13},{5,12},{6,15},{7,14},{8,1},{9,0},... | collective-permute-start | bytes 61448 | tf_op jit(solution)/shard_map/ppermute | solution.py:244
  27.1 0.0 collective-permute-done.6
  27.1 1.2 %collective-permute-done.8 = f32[40,128]{1,0:T(8,128)S(1)} collective-permute-done((f32[40,128]{1,0:T(8,128)S(1)}, f32[40,128]{1,0:T(8,128)S(1)}, u32[]{:S(2)}, u32[]{:S(2)}) %collective-permute-start.8) | collective-permute-done | bytes 20512 | tf_op jit(solution)/shard_map/ppermute | solution.py:244
  28.3 0.3 %collective-permute-done.7 = f32[40,128]{1,0:T(8,128)S(1)} collective-permute-done((f32[40,128]{1,0:T(8,128)S(1)}, f32[40,128]{1,0:T(8,128)S(1)}, u32[]{:S(2)}, u32[]{:S(2)}) %collective-permute-start.7) | collective-permute-done | bytes 20512 | tf_op jit(solution)/shard_map/ppermute | solution.py:244
  28.6 0.6 %finish.1 = (f32[32,128]{1,0:T(8,128)}, f32[1,32]{1,0:T(1,128)}) custom-call(f32[40,128]{1,0:T(8,128)S(1)} %add.22.mine_ref, f32[40,128]{1,0:T(8,128)S(1)} %add.23.theirs_ref), custom_call_target="tpu_custom_call" | custom-call | tf_op jit(solution)/shard_map/finish/pallas_call | solution.py:378
  (4 shorter events, 0.0 us)
Async XLA Ops:
  4.7 8.6 %collective-permute-start = (bf16[256,128]{1,0:T(8,128)(2,1)S(1)}, bf16[256,128]{1,0:T(8,128)(2,1)S(1)}, u32[]{:S(2)}, u32[]{:S(2)}) collective-permute-start(bf16[256,128]{1,0:T(8,128)(2,1)S(1)} %get-tuple-element.21), channel_id=1, source_target_pairs={{0,1},{1,2},{2,3},{3,4},{4,5},{5,6},{6,7},{7,0},{8,9},{9,10},{10,1... | collective-permute-start | bytes 196616 | tf_op jit(solution)/shard_map/ppermute | solution.py:267
  7.7 5.7 %collective-permute-start.1 = (bf16[256,128]{1,0:T(8,128)(2,1)S(1)}, bf16[256,128]{1,0:T(8,128)(2,1)S(1)}, u32[]{:S(2)}, u32[]{:S(2)}) collective-permute-start(bf16[256,128]{1,0:T(8,128)(2,1)S(1)} %get-tuple-element.22), channel_id=1, source_target_pairs={{0,7},{1,0},{2,1},{3,2},{4,3},{5,4},{6,5},{7,6},{8,15},{9,8},{10,9... | collective-permute-start | bytes 196616 | tf_op jit(solution)/shard_map/ppermute | solution.py:267
  15.0 3.4 %collective-permute-start.4 = (f32[40,128]{1,0:T(8,128)S(1)}, f32[40,128]{1,0:T(8,128)S(1)}, u32[]{:S(2)}, u32[]{:S(2)}) collective-permute-start(f32[40,128]{1,0:T(8,128)S(1)} %get-tuple-element.27), channel_id=1, source_target_pairs={{0,24},{1,25},{2,26},{3,27},{4,28},{5,29},{6,30},{7,31},{8,16},{9,... | collective-permute-start | bytes 61448 | tf_op jit(solution)/shard_map/ppermute | solution.py:244
  15.7 3.9 %collective-permute-start.3 = (f32[40,128]{1,0:T(8,128)S(1)}, f32[40,128]{1,0:T(8,128)S(1)}, u32[]{:S(2)}, u32[]{:S(2)}) collective-permute-start(f32[40,128]{1,0:T(8,128)S(1)} %get-tuple-element.27), channel_id=1, source_target_pairs={{0,16},{1,17},{2,18},{3,19},{4,20},{5,21},{6,22},{7,23},{8,24},{9,... | collective-permute-start | bytes 61448 | tf_op jit(solution)/shard_map/ppermute | solution.py:244
  16.7 2.9 %collective-permute-start.2 = (f32[40,128]{1,0:T(8,128)S(1)}, f32[40,128]{1,0:T(8,128)S(1)}, u32[]{:S(2)}, u32[]{:S(2)}) collective-permute-start(f32[40,128]{1,0:T(8,128)S(1)} %get-tuple-element.27), channel_id=1, source_target_pairs={{0,8},{1,9},{2,10},{3,11},{4,12},{5,13},{6,14},{7,15},{8,0},{9,1},... | collective-permute-start | bytes 61448 | tf_op jit(solution)/shard_map/ppermute | solution.py:244
  19.6 4.2 %collective-permute-start.5 = (f32[40,128]{1,0:T(8,128)S(1)}, f32[40,128]{1,0:T(8,128)S(1)}, u32[]{:S(2)}, u32[]{:S(2)}) collective-permute-start(f32[40,128]{1,0:T(8,128)S(1)} %add_add_fusion), channel_id=1, source_target_pairs={{0,12},{1,13},{2,14},{3,15},{4,8},{5,9},{6,10},{7,11},{8,4},{9,5},... | collective-permute-start | bytes 61448 | tf_op jit(solution)/shard_map/ppermute | solution.py:244
  23.8 3.3 %collective-permute-start.6 = (f32[40,128]{1,0:T(8,128)S(1)}, f32[40,128]{1,0:T(8,128)S(1)}, u32[]{:S(2)}, u32[]{:S(2)}) collective-permute-start(f32[40,128]{1,0:T(8,128)S(1)} %add.21), channel_id=1, source_target_pairs={{0,10},{1,11},{2,8},{3,9},{4,14},{5,15},{6,12},{7,13},{8,2},{9,3},... | collective-permute-start | bytes 61448 | tf_op jit(solution)/shard_map/ppermute | solution.py:244
  24.2 4.1 %collective-permute-start.8 = (f32[40,128]{1,0:T(8,128)S(1)}, f32[40,128]{1,0:T(8,128)S(1)}, u32[]{:S(2)}, u32[]{:S(2)}) collective-permute-start(f32[40,128]{1,0:T(8,128)S(1)} %add.21), channel_id=1, source_target_pairs={{0,11},{1,10},{2,9},{3,8},{4,15},{5,14},{6,13},{7,12},{8,3},{9,2},... | collective-permute-start | bytes 61448 | tf_op jit(solution)/shard_map/ppermute | solution.py:244
  25.4 3.2 %collective-permute-start.7 = (f32[40,128]{1,0:T(8,128)S(1)}, f32[40,128]{1,0:T(8,128)S(1)}, u32[]{:S(2)}, u32[]{:S(2)}) collective-permute-start(f32[40,128]{1,0:T(8,128)S(1)} %add.21), channel_id=1, source_target_pairs={{0,9},{1,8},{2,11},{3,10},{4,13},{5,12},{6,15},{7,14},{8,1},{9,0},... | collective-permute-start | bytes 61448 | tf_op jit(solution)/shard_map/ppermute | solution.py:244

commit v5 on v4

--- a/solution.py
+++ b/solution.py
@@ -47,7 +47,7 @@
     span,
     live_ref,
     latent_hbm,
-    head_hbm,
+    head_given,
     bias_hbm,
     targets_hbm,
     cell_hbm,
@@ -65,6 +65,8 @@
     targets_ref,
     predicted,
     wide_targets,
+    placed,
+    columns,
     sems,
 ):
     copies = [
@@ -72,7 +74,6 @@
         for i, (source, target) in enumerate(
             (
                 (latent_hbm, latent_ref),
-                (head_hbm, head_ref),
                 (bias_hbm, bias_ref),
                 (cell_hbm, cell_ref),
                 (pixel_hbm, pixel_ref),
@@ -88,9 +89,10 @@
     frame_width = 2 * tile_cols
     rim = tile_cols // 2
     frame_ref[...] = jnp.zeros_like(frame_ref)
-    for copy in copies[:]:
+    for copy in copies:
         copy.wait()
     bias = jnp.sum(jnp.where(eye(variables), bias_ref[...], 0.0), axis=1, keepdims=True)
+    head_ref[...] = head_given[...]
     for c in range(cycles):
         predicted[c * variables : (c + 1) * variables, :] = (
             dot(head_ref[...], latent_ref[c], NT) + bias
@@ -107,11 +109,9 @@
         weight = weight_ref[:, pl.ds(start, span)]
         gathered = dot(predicted[...], low_one_hot(cell, low_cells), NN)
         share = pick_group(gathered, cell // low_cells, cycles) * weight
-        frame_ref[...] += dot(
-            spread_groups(share, pixel // frame_width, tile_rows),
-            low_one_hot(pixel, frame_width),
-            NT,
-        )
+        placed[:, pl.ds(start, span)] = spread_groups(share, pixel // frame_width, tile_rows)
+        columns[:, pl.ds(start, span)] = low_one_hot(pixel, frame_width)
+    frame_ref[...] += dot(placed[...], columns[...], NT)
     west_ref[...] = frame_ref[:, :tile_cols].astype(BF16)
     east_ref[...] = frame_ref[:, tile_cols:].astype(BF16)
 
@@ -292,23 +292,28 @@
             jax.ShapeDtypeStruct(cell.shape, jnp.int32),
             jax.ShapeDtypeStruct(cell.shape, F32),
         ),
-        in_specs=[pl.BlockSpec(memory_space=pltpu.SMEM)] + [hbm] * 7,
+        in_specs=[pl.BlockSpec(memory_space=pltpu.SMEM), hbm, vmem, hbm, hbm, hbm, hbm, hbm],
         out_specs=[vmem] * 8,
         scratch_shapes=[
             pltpu.VMEM((1, variables), F32),
             pltpu.VMEM(targets.shape, BF16),
             pltpu.VMEM(cell_shape, BF16),
             pltpu.VMEM((variables, tile_rows, tile_cols), F32),
-            pltpu.SemaphoreType.DMA((7,)),
+            pltpu.VMEM((frame_shape[0], cell.shape[1]), BF16),
+            pltpu.VMEM((frame_shape[1], cell.shape[1]), BF16),
+            pltpu.SemaphoreType.DMA((6,)),
         ],
         compiler_params=params,
         name="forward",
     )(
         live_count,
-        *(
-            pltpu.with_memory_space_constraint(array, pltpu.HBM)
-            for array in (latent, head.T, bias.reshape(1, -1), targets, cell, pixel, weight)
-        ),
+        pltpu.with_memory_space_constraint(latent, pltpu.HBM),
+        head.T,
+        pltpu.with_memory_space_constraint(bias.reshape(1, -1), pltpu.HBM),
+        pltpu.with_memory_space_constraint(targets, pltpu.HBM),
+        pltpu.with_memory_space_constraint(cell, pltpu.HBM),
+        pltpu.with_memory_space_constraint(pixel, pltpu.HBM),
+        pltpu.with_memory_space_constraint(weight, pltpu.HBM),
     )
     from_west = from_behind(east, "lon", 1)
     from_east = from_behind(west, "lon", -1)

time: 29.4 us -> 29.4 us (level)
  starting transfers between devices: 12.8 us -> 12.4 us
  waiting for transfers between devices: 5.05 us -> 5.44 us
    ppermute x7, waiting for transfers between devices: 4.95 us -> 5.34 us  [swap(): return lax.ppermute(shard, ('lat', 'lon'), pairs)]
    ppermute x7, starting transfers between devices: 6.65 us -> 6.29 us  [swap(): return lax.ppermute(shard, ('lat', 'lon'), pairs)]
  transfers between devices with their start and end apart: 9 -> 9, of which waited for: 6 -> 7; matrix products, arithmetic and copies ran while one was open for 0% -> 0% of each run, Pallas kernels for 15% -> 15%
where the time goes in v5:
time: 29.4 us; the launch traced here: 29.2 us
  starting transfers between devices  12.4 us (42%)
  Pallas kernels  9.96 us (34%)
  waiting for transfers between devices  5.44 us (19%)
  between operations  1.35 us (5%)
    ppermute x7, starting transfers between devices, swap(): return lax.ppermute(shard, ('lat', 'lon'), pairs)  6.29 us
    ppermute x2, starting transfers between devices, from_behind(): lax.ppermute(shard, axis, [(i, (i + by) % devices) for i in range(devices)])  6.12 us
    ppermute x7, waiting for transfers between devices, swap(): return lax.ppermute(shard, ('lat', 'lon'), pairs)  5.34 us
    pallas_call x1, Pallas kernels, per_device(): pl.pallas_call(functools.partial(forward_kernel, span), out_shape=(jax.Sh...  3.31 us
    pallas_call x1, Pallas kernels, per_device(): pl.pallas_call(functools.partial(gather_latent_kernel, span), out_shape=j...  2.45 us
    pallas_call x1, Pallas kernels, per_device(): pl.pallas_call(functools.partial(backward_kernel, span, tile_rows), out_s...  1.65 us
    pallas_call x1, Pallas kernels, grad_of_latent(): pl.pallas_call(latent_kernel, out_shape=jax.ShapeDtypeStruct(latent.shape...  1.17 us
    pallas_call x1, Pallas kernels, add_early_cells(): pl.pallas_call(functools.partial(cell_kernel, span), out_shape=jax.ShapeD...  0.76 us
  transfers between devices with their start and end apart: 9, of which 7 were waited for; matrix products, arithmetic and copies ran while one was open for 0% of the time, Pallas kernels for 15%

profile of v5, /device:TPU:0, one launch (start us, length us, event | category | flops | bytes accessed | tf_op | source)
XLA Modules:
  0.0 29.2 jit_solution(9884724275113394694)
XLA Ops:
  0.6 0.0 copy-start
  1.3 0.0 copy-done
  1.3 3.3 %forward.1 = (f32[256,256]{1,0:T(8,128)S(1)}, bf16[256,128]{1,0:T(8,128)(2,1)S(1)}, bf16[256,128]{1,0:T(8,128)(2,1)S(1)}, bf16[8,256,128]{2,1,0:T(8,128)(2,1)S(1...) custom-call(s32[1,1]{1,0:T(1,128)S(6)} %copy.11.live_ref, ...), custom_call_target="tpu_custom_call" | custom-call | tf_op jit(solution)/shard_map/forward/pallas_call | solution.py:283
  4.6 3.0 %collective-permute-start = (bf16[256,128]{1,0:T(8,128)(2,1)S(1)}, bf16[256,128]{1,0:T(8,128)(2,1)S(1)}, u32[]{:S(2)}, u32[]{:S(2)}) collective-permute-start(bf16[256,128]{1,0:T(8,128)(2,1)S(1)} %get-tuple-element.21), channel_id=1, source_target_pairs={{0,1},{1,2},{2,3},{3,4},{4,5},{5,6},{6,7},{7,0},{8,9},{9,10},{10,1... | collective-permute-start | bytes 196616 | tf_op jit(solution)/shard_map/ppermute | solution.py:267
  7.7 3.1 %collective-permute-start.1 = (bf16[256,128]{1,0:T(8,128)(2,1)S(1)}, bf16[256,128]{1,0:T(8,128)(2,1)S(1)}, u32[]{:S(2)}, u32[]{:S(2)}) collective-permute-start(bf16[256,128]{1,0:T(8,128)(2,1)S(1)} %get-tuple-element.22), channel_id=1, source_target_pairs={{0,7},{1,0},{2,1},{3,2},{4,3},{5,4},{6,5},{7,6},{8,15},{9,8},{10,9... | collective-permute-start | bytes 196616 | tf_op jit(solution)/shard_map/ppermute | solution.py:267
  10.8 2.5 %gather_latent.1.row_latent_ref = bf16[128,4096]{1,0:T(8,128)(2,1)S(1)} custom-call(bf16[8,256,128]{2,1,0:T(8,128)(2,1)S(1)} %get-tuple-element.23.latent_ref, s32[1,6144]{1,0:T(1,128)S(1)} %get-tuple-element.24.cell_ref), custom_call_target="tpu_custom_call" | custom-call | flops 2147483648 | bytes 1048576 | tf_op jit(solution)/shard_map/gather_latent/pallas_call | solution.py:322
  13.2 0.0 collective-permute-done.from_west_ref
  13.2 0.1 collective-permute-done.1.from_east_ref
  13.3 1.7 %backward.1 = (bf16[32,4096]{1,0:T(8,128)(2,1)S(1)}, f32[256,256]{1,0:T(8,128)S(1)}, f32[40,128]{1,0:T(8,128)S(1)}) custom-call(f32[256,256]{1,0:T(8,128)S(1)} %get-tuple-element.20.frame_ref, bf16[256,128]{1,0:T(8,128)(2,1)S(1)} %collective-permute-done.from_west_ref, bf16[256,128]{1,0:T(8,128)(2,1)S(1)} %collective-permute-done.1.from_east_ref, ...), custom_call_target="tpu_custom_call" | custom-call | tf_op jit(solution)/shard_map/backward/pallas_call | solution.py:336
  15.0 0.6 %collective-permute-start.4 = (f32[40,128]{1,0:T(8,128)S(1)}, f32[40,128]{1,0:T(8,128)S(1)}, u32[]{:S(2)}, u32[]{:S(2)}) collective-permute-start(f32[40,128]{1,0:T(8,128)S(1)} %get-tuple-element.27), channel_id=1, source_target_pairs={{0,24},{1,25},{2,26},{3,27},{4,28},{5,29},{6,30},{7,31},{8,16},{9,... | collective-permute-start | bytes 61448 | tf_op jit(solution)/shard_map/ppermute | solution.py:244
  15.6 1.0 %collective-permute-start.3 = (f32[40,128]{1,0:T(8,128)S(1)}, f32[40,128]{1,0:T(8,128)S(1)}, u32[]{:S(2)}, u32[]{:S(2)}) collective-permute-start(f32[40,128]{1,0:T(8,128)S(1)} %get-tuple-element.27), channel_id=1, source_target_pairs={{0,16},{1,17},{2,18},{3,19},{4,20},{5,21},{6,22},{7,23},{8,24},{9,... | collective-permute-start | bytes 61448 | tf_op jit(solution)/shard_map/ppermute | solution.py:244
  16.6 0.3 collective-permute-start.2
  16.9 0.8 %cells.1.cell_misfit_ref = bf16[256,256]{1,0:T(8,128)(2,1)S(1)} custom-call(bf16[32,4096]{1,0:T(8,128)(2,1)S(1)} %get-tuple-element.28.share_ref, s32[1,6144]{1,0:T(1,128)S(1)} %get-tuple-element.24.cell_ref, f32[256,256]{1,0:T(8,128)S(1)} %get-tuple-element.29.late_ref), custom_call_target="tpu_custom_call" | custom-call | flops 805306368 | bytes 393216 | tf_op jit(solution)/shard_map/cells/pallas_call | solution.py:351
  17.7 0.7 %collective-permute-done.4 = f32[40,128]{1,0:T(8,128)S(1)} collective-permute-done((f32[40,128]{1,0:T(8,128)S(1)}, f32[40,128]{1,0:T(8,128)S(1)}, u32[]{:S(2)}, u32[]{:S(2)}) %collective-permute-start.4) | collective-permute-done | bytes 20512 | tf_op jit(solution)/shard_map/ppermute | solution.py:244
  18.4 1.1 %collective-permute-done.3 = f32[40,128]{1,0:T(8,128)S(1)} collective-permute-done((f32[40,128]{1,0:T(8,128)S(1)}, f32[40,128]{1,0:T(8,128)S(1)}, u32[]{:S(2)}, u32[]{:S(2)}) %collective-permute-start.3) | collective-permute-done | bytes 20512 | tf_op jit(solution)/shard_map/ppermute | solution.py:244
  19.5 0.0 collective-permute-done.2
  19.6 1.4 %collective-permute-start.5 = (f32[40,128]{1,0:T(8,128)S(1)}, f32[40,128]{1,0:T(8,128)S(1)}, u32[]{:S(2)}, u32[]{:S(2)}) collective-permute-start(f32[40,128]{1,0:T(8,128)S(1)} %add_add_fusion), channel_id=1, source_target_pairs={{0,12},{1,13},{2,14},{3,15},{4,8},{5,9},{6,10},{7,11},{8,4},{9,5},... | collective-permute-start | bytes 61448 | tf_op jit(solution)/shard_map/ppermute | solution.py:244
  21.0 1.2 %latent_gradient.1 = bf16[8,256,128]{2,1,0:T(8,128)(2,1)} custom-call(bf16[256,256]{1,0:T(8,128)(2,1)S(1)} %cells.1.cell_misfit_ref, bf16[32,128]{1,0:T(8,128)(2,1)S(1)} %get-tuple-element.32.head_ref), custom_call_target="tpu_custom_call" | custom-call | flops 16777216 | bytes 524288 | tf_op jit(solution)/shard_map/latent_gradient/pallas_call | solution.py:367
  22.2 2.0 %collective-permute-done.5 = f32[40,128]{1,0:T(8,128)S(1)} collective-permute-done((f32[40,128]{1,0:T(8,128)S(1)}, f32[40,128]{1,0:T(8,128)S(1)}, u32[]{:S(2)}, u32[]{:S(2)}) %collective-permute-start.5) | collective-permute-done | bytes 20512 | tf_op jit(solution)/shard_map/ppermute | solution.py:244
  24.2 0.0 collective-permute-start.6
  24.2 1.2 %collective-permute-start.8 = (f32[40,128]{1,0:T(8,128)S(1)}, f32[40,128]{1,0:T(8,128)S(1)}, u32[]{:S(2)}, u32[]{:S(2)}) collective-permute-start(f32[40,128]{1,0:T(8,128)S(1)} %add.21), channel_id=1, source_target_pairs={{0,11},{1,10},{2,9},{3,8},{4,15},{5,14},{6,13},{7,12},{8,3},{9,2},... | collective-permute-start | bytes 61448 | tf_op jit(solution)/shard_map/ppermute | solution.py:244
  25.3 1.8 %collective-permute-start.7 = (f32[40,128]{1,0:T(8,128)S(1)}, f32[40,128]{1,0:T(8,128)S(1)}, u32[]{:S(2)}, u32[]{:S(2)}) collective-permute-start(f32[40,128]{1,0:T(8,128)S(1)} %add.21), channel_id=1, source_target_pairs={{0,9},{1,8},{2,11},{3,10},{4,13},{5,12},{6,15},{7,14},{8,1},{9,0},... | collective-permute-start | bytes 61448 | tf_op jit(solution)/shard_map/ppermute | solution.py:244
  27.1 0.3 collective-permute-done.6
  27.4 1.0 %collective-permute-done.8 = f32[40,128]{1,0:T(8,128)S(1)} collective-permute-done((f32[40,128]{1,0:T(8,128)S(1)}, f32[40,128]{1,0:T(8,128)S(1)}, u32[]{:S(2)}, u32[]{:S(2)}) %collective-permute-start.8) | collective-permute-done | bytes 20512 | tf_op jit(solution)/shard_map/ppermute | solution.py:244
  28.4 0.2 collective-permute-done.7
  28.6 0.6 %finish.1 = (f32[32,128]{1,0:T(8,128)}, f32[1,32]{1,0:T(1,128)}) custom-call(f32[40,128]{1,0:T(8,128)S(1)} %add.22.mine_ref, f32[40,128]{1,0:T(8,128)S(1)} %add.23.theirs_ref), custom_call_target="tpu_custom_call" | custom-call | tf_op jit(solution)/shard_map/finish/pallas_call | solution.py:383
  (4 shorter events, 0.0 us)
Async XLA Ops:
  0.6 0.7 %copy-start = (bf16[128,32]{0,1:T(8,128)(2,1)S(1)}, bf16[128,32]{0,1:T(8,128)(2,1)}, u32[]{:S(2)}) copy-start(bf16[128,32]{0,1:T(8,128)(2,1)} %param.9) | copy-start | bytes 24580
  4.6 8.6 %collective-permute-start = (bf16[256,128]{1,0:T(8,128)(2,1)S(1)}, bf16[256,128]{1,0:T(8,128)(2,1)S(1)}, u32[]{:S(2)}, u32[]{:S(2)}) collective-permute-start(bf16[256,128]{1,0:T(8,128)(2,1)S(1)} %get-tuple-element.21), channel_id=1, source_target_pairs={{0,1},{1,2},{2,3},{3,4},{4,5},{5,6},{6,7},{7,0},{8,9},{9,10},{10,1... | collective-permute-start | bytes 196616 | tf_op jit(solution)/shard_map/ppermute | solution.py:267
  7.7 5.7 %collective-permute-start.1 = (bf16[256,128]{1,0:T(8,128)(2,1)S(1)}, bf16[256,128]{1,0:T(8,128)(2,1)S(1)}, u32[]{:S(2)}, u32[]{:S(2)}) collective-permute-start(bf16[256,128]{1,0:T(8,128)(2,1)S(1)} %get-tuple-element.22), channel_id=1, source_target_pairs={{0,7},{1,0},{2,1},{3,2},{4,3},{5,4},{6,5},{7,6},{8,15},{9,8},{10,9... | collective-permute-start | bytes 196616 | tf_op jit(solution)/shard_map/ppermute | solution.py:267
  15.0 3.4 %collective-permute-start.4 = (f32[40,128]{1,0:T(8,128)S(1)}, f32[40,128]{1,0:T(8,128)S(1)}, u32[]{:S(2)}, u32[]{:S(2)}) collective-permute-start(f32[40,128]{1,0:T(8,128)S(1)} %get-tuple-element.27), channel_id=1, source_target_pairs={{0,24},{1,25},{2,26},{3,27},{4,28},{5,29},{6,30},{7,31},{8,16},{9,... | collective-permute-start | bytes 61448 | tf_op jit(solution)/shard_map/ppermute | solution.py:244
  15.6 3.9 %collective-permute-start.3 = (f32[40,128]{1,0:T(8,128)S(1)}, f32[40,128]{1,0:T(8,128)S(1)}, u32[]{:S(2)}, u32[]{:S(2)}) collective-permute-start(f32[40,128]{1,0:T(8,128)S(1)} %get-tuple-element.27), channel_id=1, source_target_pairs={{0,16},{1,17},{2,18},{3,19},{4,20},{5,21},{6,22},{7,23},{8,24},{9,... | collective-permute-start | bytes 61448 | tf_op jit(solution)/shard_map/ppermute | solution.py:244
  16.6 2.9 %collective-permute-start.2 = (f32[40,128]{1,0:T(8,128)S(1)}, f32[40,128]{1,0:T(8,128)S(1)}, u32[]{:S(2)}, u32[]{:S(2)}) collective-permute-start(f32[40,128]{1,0:T(8,128)S(1)} %get-tuple-element.27), channel_id=1, source_target_pairs={{0,8},{1,9},{2,10},{3,11},{4,12},{5,13},{6,14},{7,15},{8,0},{9,1},... | collective-permute-start | bytes 61448 | tf_op jit(solution)/shard_map/ppermute | solution.py:244
  19.6 4.6 %collective-permute-start.5 = (f32[40,128]{1,0:T(8,128)S(1)}, f32[40,128]{1,0:T(8,128)S(1)}, u32[]{:S(2)}, u32[]{:S(2)}) collective-permute-start(f32[40,128]{1,0:T(8,128)S(1)} %add_add_fusion), channel_id=1, source_target_pairs={{0,12},{1,13},{2,14},{3,15},{4,8},{5,9},{6,10},{7,11},{8,4},{9,5},... | collective-permute-start | bytes 61448 | tf_op jit(solution)/shard_map/ppermute | solution.py:244
  24.2 3.2 %collective-permute-start.6 = (f32[40,128]{1,0:T(8,128)S(1)}, f32[40,128]{1,0:T(8,128)S(1)}, u32[]{:S(2)}, u32[]{:S(2)}) collective-permute-start(f32[40,128]{1,0:T(8,128)S(1)} %add.21), channel_id=1, source_target_pairs={{0,10},{1,11},{2,8},{3,9},{4,14},{5,15},{6,12},{7,13},{8,2},{9,3},... | collective-permute-start | bytes 61448 | tf_op jit(solution)/shard_map/ppermute | solution.py:244
  24.2 4.2 %collective-permute-start.8 = (f32[40,128]{1,0:T(8,128)S(1)}, f32[40,128]{1,0:T(8,128)S(1)}, u32[]{:S(2)}, u32[]{:S(2)}) collective-permute-start(f32[40,128]{1,0:T(8,128)S(1)} %add.21), channel_id=1, source_target_pairs={{0,11},{1,10},{2,9},{3,8},{4,15},{5,14},{6,13},{7,12},{8,3},{9,2},... | collective-permute-start | bytes 61448 | tf_op jit(solution)/shard_map/ppermute | solution.py:244
  25.3 3.3 %collective-permute-start.7 = (f32[40,128]{1,0:T(8,128)S(1)}, f32[40,128]{1,0:T(8,128)S(1)}, u32[]{:S(2)}, u32[]{:S(2)}) collective-permute-start(f32[40,128]{1,0:T(8,128)S(1)} %add.21), channel_id=1, source_target_pairs={{0,9},{1,8},{2,11},{3,10},{4,13},{5,12},{6,15},{7,14},{8,1},{9,0},... | collective-permute-start | bytes 61448 | tf_op jit(solution)/shard_map/ppermute | solution.py:244

commit v6 on v5

--- a/solution.py
+++ b/solution.py
@@ -218,13 +218,14 @@
     low_first = [1 << k for k in range(lat.bit_length() - 1)]
     while low_first:
         pair, low_first = low_first[:2], low_first[2:]
-        rounds.append([(s, 0) for s in pair + [pair[0] ^ pair[-1]] * (len(pair) - 1)])
+        flips = pair + [pair[0] ^ pair[-1]] * (len(pair) - 1)
+        rounds.append([(s, 0) for s in flips[1:] + flips[:1]])
     cross = min(lat - 1, 1)
     high_first = [1 << k for k in reversed(range(lon.bit_length() - 1))]
     while high_first:
         take = 2 - len(high_first) % 2
         pair, high_first = high_first[:take], high_first[take:]
-        rounds.append([(cross, s) for s in pair + [pair[0] ^ pair[-1]] * (take - 1)])
+        rounds.append([(cross, s) for s in [pair[0] ^ pair[-1]] * (take - 1) + pair])
     return rounds
 
 
@@ -241,13 +242,14 @@
         pairs = [
             (i * lon + j, (i ^ flip[0]) * lon + (j ^ flip[1])) for i in range(lat) for j in range(lon)
         ]
-        return lax.ppermute(shard, ("lat", "lon"), pairs)
+        return lax.ppermute(shard, ("lat", "lon"), pairs).astype(F32)
 
     jobs, done = list(jobs), None
     powers = lat & (lat - 1) == 0 and lon & (lon - 1) == 0
     rounds = sum_rounds(lat, lon) if powers else []
     for flips in rounds[:-1]:
-        shards = [value] + [swap(value, flip) for flip in flips]
+        narrow = value.astype(BF16)
+        shards = [narrow.astype(F32)] + [swap(narrow, flip) for flip in flips]
         if jobs:
             done = jobs.pop(0)(done)
             value, done = lax.optimization_barrier((add_pairs(shards), done))
@@ -257,7 +259,8 @@
         done = job(done)
     if not rounds:
         return lax.psum(value, ("lat", "lon")), jnp.zeros_like(value), done
-    last = [value] + [swap(value, flip) for flip in rounds[-1]]
+    narrow = value.astype(BF16)
+    last = [narrow.astype(F32)] + [swap(narrow, flip) for flip in rounds[-1]]
     half = len(last) // 2
     return add_pairs(last[:half]), add_pairs(last[half:]), done
 

time: 29.4 us -> 29.2 us (level)
  waiting for transfers between devices: 5.44 us -> 5.03 us
    ppermute x7, waiting for transfers between devices: 5.34 us -> 4.93 us  [swap(): return lax.ppermute(shard, ('lat', 'lon'), pairs).astype(F32)]
where the time goes in v6:
time: 29.2 us; the launch traced here: 28.9 us
  starting transfers between devices  12.5 us (43%)
  Pallas kernels  9.96 us (34%)
  waiting for transfers between devices  5.03 us (17%)
  between operations  1.35 us (5%)
    ppermute x7, starting transfers between devices, swap(): return lax.ppermute(shard, ('lat', 'lon'), pairs).astype(F32)  6.39 us
    ppermute x2, starting transfers between devices, from_behind(): lax.ppermute(shard, axis, [(i, (i + by) % devices) for i in range(devices)])  6.12 us
    ppermute x7, waiting for transfers between devices, swap(): return lax.ppermute(shard, ('lat', 'lon'), pairs).astype(F32)  4.93 us
    pallas_call x1, Pallas kernels, per_device(): pl.pallas_call(functools.partial(forward_kernel, span), out_shape=(jax.Sh...  3.31 us
    pallas_call x1, Pallas kernels, per_device(): pl.pallas_call(functools.partial(gather_latent_kernel, span), out_shape=j...  2.45 us
    pallas_call x1, Pallas kernels, per_device(): pl.pallas_call(functools.partial(backward_kernel, span, tile_rows), out_s...  1.65 us
    pallas_call x1, Pallas kernels, grad_of_latent(): pl.pallas_call(latent_kernel, out_shape=jax.ShapeDtypeStruct(latent.shape...  1.17 us
    pallas_call x1, Pallas kernels, add_early_cells(): pl.pallas_call(functools.partial(cell_kernel, span), out_shape=jax.ShapeD...  0.77 us
  transfers between devices with their start and end apart: 9, of which 7 were waited for; matrix products, arithmetic and copies ran while one was open for 0% of the time, Pallas kernels for 15%

profile of v6, /device:TPU:0, one launch (start us, length us, event | category | flops | bytes accessed | tf_op | source)
XLA Modules:
  0.0 28.9 jit_solution(6288823772204078348)
XLA Ops:
  0.6 0.0 copy-start
  1.3 0.0 copy-done
  1.3 3.3 %forward.1 = (f32[256,256]{1,0:T(8,128)S(1)}, bf16[256,128]{1,0:T(8,128)(2,1)S(1)}, bf16[256,128]{1,0:T(8,128)(2,1)S(1)}, bf16[8,256,128]{2,1,0:T(8,128)(2,1)S(1...) custom-call(s32[1,1]{1,0:T(1,128)S(6)} %copy.11.live_ref, ...), custom_call_target="tpu_custom_call" | custom-call | tf_op jit(solution)/shard_map/forward/pallas_call | solution.py:286
  4.6 3.0 %collective-permute-start = (bf16[256,128]{1,0:T(8,128)(2,1)S(1)}, bf16[256,128]{1,0:T(8,128)(2,1)S(1)}, u32[]{:S(2)}, u32[]{:S(2)}) collective-permute-start(bf16[256,128]{1,0:T(8,128)(2,1)S(1)} %get-tuple-element.21), channel_id=1, source_target_pairs={{0,1},{1,2},{2,3},{3,4},{4,5},{5,6},{6,7},{7,0},{8,9},{9,10},{10,1... | collective-permute-start | bytes 196616 | tf_op jit(solution)/shard_map/ppermute | solution.py:270
  7.7 3.1 %collective-permute-start.1 = (bf16[256,128]{1,0:T(8,128)(2,1)S(1)}, bf16[256,128]{1,0:T(8,128)(2,1)S(1)}, u32[]{:S(2)}, u32[]{:S(2)}) collective-permute-start(bf16[256,128]{1,0:T(8,128)(2,1)S(1)} %get-tuple-element.22), channel_id=1, source_target_pairs={{0,7},{1,0},{2,1},{3,2},{4,3},{5,4},{6,5},{7,6},{8,15},{9,8},{10,9... | collective-permute-start | bytes 196616 | tf_op jit(solution)/shard_map/ppermute | solution.py:270
  10.8 2.5 %gather_latent.1.row_latent_ref = bf16[128,4096]{1,0:T(8,128)(2,1)S(1)} custom-call(bf16[8,256,128]{2,1,0:T(8,128)(2,1)S(1)} %get-tuple-element.23.latent_ref, s32[1,6144]{1,0:T(1,128)S(1)} %get-tuple-element.24.cell_ref), custom_call_target="tpu_custom_call" | custom-call | flops 2147483648 | bytes 1048576 | tf_op jit(solution)/shard_map/gather_latent/pallas_call | solution.py:325
  13.2 0.0 collective-permute-done.from_west_ref
  13.2 0.1 collective-permute-done.1.from_east_ref
  13.3 1.7 %backward.1 = (bf16[32,4096]{1,0:T(8,128)(2,1)S(1)}, f32[256,256]{1,0:T(8,128)S(1)}, f32[40,128]{1,0:T(8,128)S(1)}) custom-call(f32[256,256]{1,0:T(8,128)S(1)} %get-tuple-element.20.frame_ref, bf16[256,128]{1,0:T(8,128)(2,1)S(1)} %collective-permute-done.from_west_ref, bf16[256,128]{1,0:T(8,128)(2,1)S(1)} %collective-permute-done.1.from_east_ref, ...), custom_call_target="tpu_custom_call" | custom-call | tf_op jit(solution)/shard_map/backward/pallas_call | solution.py:339
  15.0 0.6 %collective-permute-start.3 = (bf16[40,128]{1,0:T(8,128)(2,1)S(1)}, bf16[40,128]{1,0:T(8,128)(2,1)S(1)}, u32[]{:S(2)}, u32[]{:S(2)}) collective-permute-start(bf16[40,128]{1,0:T(8,128)(2,1)S(1)} %convert_element_type.39), channel_id=1, source_target_pairs={{0,24},{1,25},{2,26},{3,27},{4,28},{5,29},{6,30},{7,31},{8,16},{9,... | collective-permute-start | bytes 30728 | tf_op jit(solution)/shard_map/ppermute | solution.py:245
  15.7 1.0 %collective-permute-start.2 = (bf16[40,128]{1,0:T(8,128)(2,1)S(1)}, bf16[40,128]{1,0:T(8,128)(2,1)S(1)}, u32[]{:S(2)}, u32[]{:S(2)}) collective-permute-start(bf16[40,128]{1,0:T(8,128)(2,1)S(1)} %convert_element_type.39), channel_id=1, source_target_pairs={{0,16},{1,17},{2,18},{3,19},{4,20},{5,21},{6,22},{7,23},{8,24},{9,... | collective-permute-start | bytes 30728 | tf_op jit(solution)/shard_map/ppermute | solution.py:245
  16.7 0.3 collective-permute-start.4
  17.0 0.8 %cells.1.cell_misfit_ref = bf16[256,256]{1,0:T(8,128)(2,1)S(1)} custom-call(bf16[32,4096]{1,0:T(8,128)(2,1)S(1)} %get-tuple-element.28.share_ref, s32[1,6144]{1,0:T(1,128)S(1)} %get-tuple-element.24.cell_ref, f32[256,256]{1,0:T(8,128)S(1)} %get-tuple-element.29.late_ref), custom_call_target="tpu_custom_call" | custom-call | flops 805306368 | bytes 393216 | tf_op jit(solution)/shard_map/cells/pallas_call | solution.py:354
  17.7 0.5 %collective-permute-done.3 = bf16[40,128]{1,0:T(8,128)(2,1)S(1)} collective-permute-done((bf16[40,128]{1,0:T(8,128)(2,1)S(1)}, bf16[40,128]{1,0:T(8,128)(2,1)S(1)}, u32[]{:S(2)}, u32[]{:S(2)}) %collective-permute-start.3) | collective-permute-done | bytes 10272 | tf_op jit(solution)/shard_map/ppermute | solution.py:245
  18.2 1.1 %collective-permute-done.2 = bf16[40,128]{1,0:T(8,128)(2,1)S(1)} collective-permute-done((bf16[40,128]{1,0:T(8,128)(2,1)S(1)}, bf16[40,128]{1,0:T(8,128)(2,1)S(1)}, u32[]{:S(2)}, u32[]{:S(2)}) %collective-permute-start.2) | collective-permute-done | bytes 10272 | tf_op jit(solution)/shard_map/ppermute | solution.py:245
  19.4 0.0 collective-permute-done.4
  19.4 1.4 %collective-permute-start.5 = (bf16[40,128]{1,0:T(8,128)(2,1)S(1)}, bf16[40,128]{1,0:T(8,128)(2,1)S(1)}, u32[]{:S(2)}, u32[]{:S(2)}) collective-permute-start(bf16[40,128]{1,0:T(8,128)(2,1)S(1)} %add_add_fusion), channel_id=1, source_target_pairs={{0,12},{1,13},{2,14},{3,15},{4,8},{5,9},{6,10},{7,11},{8,4},{9,5},... | collective-permute-start | bytes 30728 | tf_op jit(solution)/shard_map/ppermute | solution.py:245
  20.8 1.2 %latent_gradient.1 = bf16[8,256,128]{2,1,0:T(8,128)(2,1)} custom-call(bf16[256,256]{1,0:T(8,128)(2,1)S(1)} %cells.1.cell_misfit_ref, bf16[32,128]{1,0:T(8,128)(2,1)S(1)} %get-tuple-element.32.head_ref), custom_call_target="tpu_custom_call" | custom-call | flops 16777216 | bytes 524288 | tf_op jit(solution)/shard_map/latent_gradient/pallas_call | solution.py:370
  22.0 1.5 %collective-permute-done.5 = bf16[40,128]{1,0:T(8,128)(2,1)S(1)} collective-permute-done((bf16[40,128]{1,0:T(8,128)(2,1)S(1)}, bf16[40,128]{1,0:T(8,128)(2,1)S(1)}, u32[]{:S(2)}, u32[]{:S(2)}) %collective-permute-start.5) | collective-permute-done | bytes 10272 | tf_op jit(solution)/shard_map/ppermute | solution.py:245
  23.4 1.7 %collective-permute-start.6 = (bf16[40,128]{1,0:T(8,128)(2,1)S(1)}, bf16[40,128]{1,0:T(8,128)(2,1)S(1)}, u32[]{:S(2)}, u32[]{:S(2)}) collective-permute-start(bf16[40,128]{1,0:T(8,128)(2,1)S(1)} %convert_add_fusion.2), channel_id=1, source_target_pairs={{0,11},{1,10},{2,9},{3,8},{4,15},{5,14},{6,13},{7,12},{8,3},{9,2},... | collective-permute-start | bytes 30728 | tf_op jit(solution)/shard_map/ppermute | solution.py:245
  25.1 0.1 collective-permute-start.7
  25.2 1.2 %collective-permute-start.8 = (bf16[40,128]{1,0:T(8,128)(2,1)S(1)}, bf16[40,128]{1,0:T(8,128)(2,1)S(1)}, u32[]{:S(2)}, u32[]{:S(2)}) collective-permute-start(bf16[40,128]{1,0:T(8,128)(2,1)S(1)} %convert_add_fusion.2), channel_id=1, source_target_pairs={{0,9},{1,8},{2,11},{3,10},{4,13},{5,12},{6,15},{7,14},{8,1},{9,0},... | collective-permute-start | bytes 30728 | tf_op jit(solution)/shard_map/ppermute | solution.py:245
  26.5 1.0 %collective-permute-done.6 = bf16[40,128]{1,0:T(8,128)(2,1)S(1)} collective-permute-done((bf16[40,128]{1,0:T(8,128)(2,1)S(1)}, bf16[40,128]{1,0:T(8,128)(2,1)S(1)}, u32[]{:S(2)}, u32[]{:S(2)}) %collective-permute-start.6) | collective-permute-done | bytes 10272 | tf_op jit(solution)/shard_map/ppermute | solution.py:245
  27.5 0.7 %collective-permute-done.7 = bf16[40,128]{1,0:T(8,128)(2,1)S(1)} collective-permute-done((bf16[40,128]{1,0:T(8,128)(2,1)S(1)}, bf16[40,128]{1,0:T(8,128)(2,1)S(1)}, u32[]{:S(2)}, u32[]{:S(2)}) %collective-permute-start.7) | collective-permute-done | bytes 10272 | tf_op jit(solution)/shard_map/ppermute | solution.py:245
  28.2 0.1 collective-permute-done.8
  28.3 0.6 %finish.1 = (f32[32,128]{1,0:T(8,128)}, f32[1,32]{1,0:T(1,128)}) custom-call(f32[40,128]{1,0:T(8,128)S(1)} %convert_add_fusion.1.mine_ref, f32[40,128]{1,0:T(8,128)S(1)} %convert_add_fusion.theirs_ref), custom_call_target="tpu_custom_call" | custom-call | tf_op jit(solution)/shard_map/finish/pallas_call | solution.py:386
  (5 shorter events, 0.1 us)
Async XLA Ops:
  0.6 0.7 %copy-start = (bf16[128,32]{0,1:T(8,128)(2,1)S(1)}, bf16[128,32]{0,1:T(8,128)(2,1)}, u32[]{:S(2)}) copy-start(bf16[128,32]{0,1:T(8,128)(2,1)} %param.9) | copy-start | bytes 24580
  4.6 8.6 %collective-permute-start = (bf16[256,128]{1,0:T(8,128)(2,1)S(1)}, bf16[256,128]{1,0:T(8,128)(2,1)S(1)}, u32[]{:S(2)}, u32[]{:S(2)}) collective-permute-start(bf16[256,128]{1,0:T(8,128)(2,1)S(1)} %get-tuple-element.21), channel_id=1, source_target_pairs={{0,1},{1,2},{2,3},{3,4},{4,5},{5,6},{6,7},{7,0},{8,9},{9,10},{10,1... | collective-permute-start | bytes 196616 | tf_op jit(solution)/shard_map/ppermute | solution.py:270
  7.7 5.7 %collective-permute-start.1 = (bf16[256,128]{1,0:T(8,128)(2,1)S(1)}, bf16[256,128]{1,0:T(8,128)(2,1)S(1)}, u32[]{:S(2)}, u32[]{:S(2)}) collective-permute-start(bf16[256,128]{1,0:T(8,128)(2,1)S(1)} %get-tuple-element.22), channel_id=1, source_target_pairs={{0,7},{1,0},{2,1},{3,2},{4,3},{5,4},{6,5},{7,6},{8,15},{9,8},{10,9... | collective-permute-start | bytes 196616 | tf_op jit(solution)/shard_map/ppermute | solution.py:270
  15.0 3.2 %collective-permute-start.3 = (bf16[40,128]{1,0:T(8,128)(2,1)S(1)}, bf16[40,128]{1,0:T(8,128)(2,1)S(1)}, u32[]{:S(2)}, u32[]{:S(2)}) collective-permute-start(bf16[40,128]{1,0:T(8,128)(2,1)S(1)} %convert_element_type.39), channel_id=1, source_target_pairs={{0,24},{1,25},{2,26},{3,27},{4,28},{5,29},{6,30},{7,31},{8,16},{9,... | collective-permute-start | bytes 30728 | tf_op jit(solution)/shard_map/ppermute | solution.py:245
  15.7 3.7 %collective-permute-start.2 = (bf16[40,128]{1,0:T(8,128)(2,1)S(1)}, bf16[40,128]{1,0:T(8,128)(2,1)S(1)}, u32[]{:S(2)}, u32[]{:S(2)}) collective-permute-start(bf16[40,128]{1,0:T(8,128)(2,1)S(1)} %convert_element_type.39), channel_id=1, source_target_pairs={{0,16},{1,17},{2,18},{3,19},{4,20},{5,21},{6,22},{7,23},{8,24},{9,... | collective-permute-start | bytes 30728 | tf_op jit(solution)/shard_map/ppermute | solution.py:245
  16.7 2.7 %collective-permute-start.4 = (bf16[40,128]{1,0:T(8,128)(2,1)S(1)}, bf16[40,128]{1,0:T(8,128)(2,1)S(1)}, u32[]{:S(2)}, u32[]{:S(2)}) collective-permute-start(bf16[40,128]{1,0:T(8,128)(2,1)S(1)} %convert_element_type.39), channel_id=1, source_target_pairs={{0,8},{1,9},{2,10},{3,11},{4,12},{5,13},{6,14},{7,15},{8,0},{9,1},... | collective-permute-start | bytes 30728 | tf_op jit(solution)/shard_map/ppermute | solution.py:245
  19.4 4.1 %collective-permute-start.5 = (bf16[40,128]{1,0:T(8,128)(2,1)S(1)}, bf16[40,128]{1,0:T(8,128)(2,1)S(1)}, u32[]{:S(2)}, u32[]{:S(2)}) collective-permute-start(bf16[40,128]{1,0:T(8,128)(2,1)S(1)} %add_add_fusion), channel_id=1, source_target_pairs={{0,12},{1,13},{2,14},{3,15},{4,8},{5,9},{6,10},{7,11},{8,4},{9,5},... | collective-permute-start | bytes 30728 | tf_op jit(solution)/shard_map/ppermute | solution.py:245
  23.4 4.1 %collective-permute-start.6 = (bf16[40,128]{1,0:T(8,128)(2,1)S(1)}, bf16[40,128]{1,0:T(8,128)(2,1)S(1)}, u32[]{:S(2)}, u32[]{:S(2)}) collective-permute-start(bf16[40,128]{1,0:T(8,128)(2,1)S(1)} %convert_add_fusion.2), channel_id=1, source_target_pairs={{0,11},{1,10},{2,9},{3,8},{4,15},{5,14},{6,13},{7,12},{8,3},{9,2},... | collective-permute-start | bytes 30728 | tf_op jit(solution)/shard_map/ppermute | solution.py:245
  25.1 3.1 %collective-permute-start.7 = (bf16[40,128]{1,0:T(8,128)(2,1)S(1)}, bf16[40,128]{1,0:T(8,128)(2,1)S(1)}, u32[]{:S(2)}, u32[]{:S(2)}) collective-permute-start(bf16[40,128]{1,0:T(8,128)(2,1)S(1)} %convert_add_fusion.2), channel_id=1, source_target_pairs={{0,10},{1,11},{2,8},{3,9},{4,14},{5,15},{6,12},{7,13},{8,2},{9,3},... | collective-permute-start | bytes 30728 | tf_op jit(solution)/shard_map/ppermute | solution.py:245
  25.2 3.1 %collective-permute-start.8 = (bf16[40,128]{1,0:T(8,128)(2,1)S(1)}, bf16[40,128]{1,0:T(8,128)(2,1)S(1)}, u32[]{:S(2)}, u32[]{:S(2)}) collective-permute-start(bf16[40,128]{1,0:T(8,128)(2,1)S(1)} %convert_add_fusion.2), channel_id=1, source_target_pairs={{0,9},{1,8},{2,11},{3,10},{4,13},{5,12},{6,15},{7,14},{8,1},{9,0},... | collective-permute-start | bytes 30728 | tf_op jit(solution)/shard_map/ppermute | solution.py:245

commit v7 on v6

--- a/solution.py
+++ b/solution.py
@@ -225,7 +225,7 @@
     while high_first:
         take = 2 - len(high_first) % 2
         pair, high_first = high_first[:take], high_first[take:]
-        rounds.append([(cross, s) for s in [pair[0] ^ pair[-1]] * (take - 1) + pair])
+        rounds.append([(cross, s) for s in pair[:1] + [pair[0] ^ pair[-1]] * (take - 1) + pair[1:]])
     return rounds
 
 

time: 29.2 us -> 29.2 us (level)
  no operation moved by 1% of the time
where the time goes in v7:
time: 29.2 us; the launch traced here: 29 us
  starting transfers between devices  12.5 us (43%)
  Pallas kernels  9.96 us (34%)
  waiting for transfers between devices  5.05 us (17%)
  between operations  1.35 us (5%)
    ppermute x7, starting transfers between devices, swap(): return lax.ppermute(shard, ('lat', 'lon'), pairs).astype(F32)  6.39 us
    ppermute x2, starting transfers between devices, from_behind(): lax.ppermute(shard, axis, [(i, (i + by) % devices) for i in range(devices)])  6.12 us
    ppermute x7, waiting for transfers between devices, swap(): return lax.ppermute(shard, ('lat', 'lon'), pairs).astype(F32)  4.95 us
    pallas_call x1, Pallas kernels, per_device(): pl.pallas_call(functools.partial(forward_kernel, span), out_shape=(jax.Sh...  3.31 us
    pallas_call x1, Pallas kernels, per_device(): pl.pallas_call(functools.partial(gather_latent_kernel, span), out_shape=j...  2.45 us
    pallas_call x1, Pallas kernels, per_device(): pl.pallas_call(functools.partial(backward_kernel, span, tile_rows), out_s...  1.65 us
    pallas_call x1, Pallas kernels, grad_of_latent(): pl.pallas_call(latent_kernel, out_shape=jax.ShapeDtypeStruct(latent.shape...  1.17 us
    pallas_call x1, Pallas kernels, add_early_cells(): pl.pallas_call(functools.partial(cell_kernel, span), out_shape=jax.ShapeD...  0.77 us
  transfers between devices with their start and end apart: 9, of which 7 were waited for; matrix products, arithmetic and copies ran while one was open for 0% of the time, Pallas kernels for 15%

profile of v7, /device:TPU:0, one launch (start us, length us, event | category | flops | bytes accessed | tf_op | source)
XLA Modules:
  0.0 29.0 jit_solution(1879027781183473083)
XLA Ops:
  0.6 0.0 copy-start
  1.3 0.0 copy-done
  1.3 3.3 %forward.1 = (f32[256,256]{1,0:T(8,128)S(1)}, bf16[256,128]{1,0:T(8,128)(2,1)S(1)}, bf16[256,128]{1,0:T(8,128)(2,1)S(1)}, bf16[8,256,128]{2,1,0:T(8,128)(2,1)S(1...) custom-call(s32[1,1]{1,0:T(1,128)S(6)} %copy.11.live_ref, ...), custom_call_target="tpu_custom_call" | custom-call | tf_op jit(solution)/shard_map/forward/pallas_call | solution.py:286
  4.6 3.0 %collective-permute-start = (bf16[256,128]{1,0:T(8,128)(2,1)S(1)}, bf16[256,128]{1,0:T(8,128)(2,1)S(1)}, u32[]{:S(2)}, u32[]{:S(2)}) collective-permute-start(bf16[256,128]{1,0:T(8,128)(2,1)S(1)} %get-tuple-element.21), channel_id=1, source_target_pairs={{0,1},{1,2},{2,3},{3,4},{4,5},{5,6},{6,7},{7,0},{8,9},{9,10},{10,1... | collective-permute-start | bytes 196616 | tf_op jit(solution)/shard_map/ppermute | solution.py:270
  7.7 3.1 %collective-permute-start.1 = (bf16[256,128]{1,0:T(8,128)(2,1)S(1)}, bf16[256,128]{1,0:T(8,128)(2,1)S(1)}, u32[]{:S(2)}, u32[]{:S(2)}) collective-permute-start(bf16[256,128]{1,0:T(8,128)(2,1)S(1)} %get-tuple-element.22), channel_id=1, source_target_pairs={{0,7},{1,0},{2,1},{3,2},{4,3},{5,4},{6,5},{7,6},{8,15},{9,8},{10,9... | collective-permute-start | bytes 196616 | tf_op jit(solution)/shard_map/ppermute | solution.py:270
  10.8 2.5 %gather_latent.1.row_latent_ref = bf16[128,4096]{1,0:T(8,128)(2,1)S(1)} custom-call(bf16[8,256,128]{2,1,0:T(8,128)(2,1)S(1)} %get-tuple-element.23.latent_ref, s32[1,6144]{1,0:T(1,128)S(1)} %get-tuple-element.24.cell_ref), custom_call_target="tpu_custom_call" | custom-call | flops 2147483648 | bytes 1048576 | tf_op jit(solution)/shard_map/gather_latent/pallas_call | solution.py:325
  13.2 0.0 collective-permute-done.from_west_ref
  13.2 0.1 collective-permute-done.1.from_east_ref
  13.3 1.7 %backward.1 = (bf16[32,4096]{1,0:T(8,128)(2,1)S(1)}, f32[256,256]{1,0:T(8,128)S(1)}, f32[40,128]{1,0:T(8,128)S(1)}) custom-call(f32[256,256]{1,0:T(8,128)S(1)} %get-tuple-element.20.frame_ref, bf16[256,128]{1,0:T(8,128)(2,1)S(1)} %collective-permute-done.from_west_ref, bf16[256,128]{1,0:T(8,128)(2,1)S(1)} %collective-permute-done.1.from_east_ref, ...), custom_call_target="tpu_custom_call" | custom-call | tf_op jit(solution)/shard_map/backward/pallas_call | solution.py:339
  15.0 0.6 %collective-permute-start.3 = (bf16[40,128]{1,0:T(8,128)(2,1)S(1)}, bf16[40,128]{1,0:T(8,128)(2,1)S(1)}, u32[]{:S(2)}, u32[]{:S(2)}) collective-permute-start(bf16[40,128]{1,0:T(8,128)(2,1)S(1)} %convert_element_type.39), channel_id=1, source_target_pairs={{0,24},{1,25},{2,26},{3,27},{4,28},{5,29},{6,30},{7,31},{8,16},{9,... | collective-permute-start | bytes 30728 | tf_op jit(solution)/shard_map/ppermute | solution.py:245
  15.7 1.0 %collective-permute-start.2 = (bf16[40,128]{1,0:T(8,128)(2,1)S(1)}, bf16[40,128]{1,0:T(8,128)(2,1)S(1)}, u32[]{:S(2)}, u32[]{:S(2)}) collective-permute-start(bf16[40,128]{1,0:T(8,128)(2,1)S(1)} %convert_element_type.39), channel_id=1, source_target_pairs={{0,16},{1,17},{2,18},{3,19},{4,20},{5,21},{6,22},{7,23},{8,24},{9,... | collective-permute-start | bytes 30728 | tf_op jit(solution)/shard_map/ppermute | solution.py:245
  16.7 0.3 collective-permute-start.4
  17.0 0.8 %cells.1.cell_misfit_ref = bf16[256,256]{1,0:T(8,128)(2,1)S(1)} custom-call(bf16[32,4096]{1,0:T(8,128)(2,1)S(1)} %get-tuple-element.28.share_ref, s32[1,6144]{1,0:T(1,128)S(1)} %get-tuple-element.24.cell_ref, f32[256,256]{1,0:T(8,128)S(1)} %get-tuple-element.29.late_ref), custom_call_target="tpu_custom_call" | custom-call | flops 805306368 | bytes 393216 | tf_op jit(solution)/shard_map/cells/pallas_call | solution.py:354
  17.7 0.5 %collective-permute-done.3 = bf16[40,128]{1,0:T(8,128)(2,1)S(1)} collective-permute-done((bf16[40,128]{1,0:T(8,128)(2,1)S(1)}, bf16[40,128]{1,0:T(8,128)(2,1)S(1)}, u32[]{:S(2)}, u32[]{:S(2)}) %collective-permute-start.3) | collective-permute-done | bytes 10272 | tf_op jit(solution)/shard_map/ppermute | solution.py:245
  18.2 1.1 %collective-permute-done.2 = bf16[40,128]{1,0:T(8,128)(2,1)S(1)} collective-permute-done((bf16[40,128]{1,0:T(8,128)(2,1)S(1)}, bf16[40,128]{1,0:T(8,128)(2,1)S(1)}, u32[]{:S(2)}, u32[]{:S(2)}) %collective-permute-start.2) | collective-permute-done | bytes 10272 | tf_op jit(solution)/shard_map/ppermute | solution.py:245
  19.4 0.0 collective-permute-done.4
  19.4 1.4 %collective-permute-start.5 = (bf16[40,128]{1,0:T(8,128)(2,1)S(1)}, bf16[40,128]{1,0:T(8,128)(2,1)S(1)}, u32[]{:S(2)}, u32[]{:S(2)}) collective-permute-start(bf16[40,128]{1,0:T(8,128)(2,1)S(1)} %add_add_fusion), channel_id=1, source_target_pairs={{0,12},{1,13},{2,14},{3,15},{4,8},{5,9},{6,10},{7,11},{8,4},{9,5},... | collective-permute-start | bytes 30728 | tf_op jit(solution)/shard_map/ppermute | solution.py:245
  20.8 1.2 %latent_gradient.1 = bf16[8,256,128]{2,1,0:T(8,128)(2,1)} custom-call(bf16[256,256]{1,0:T(8,128)(2,1)S(1)} %cells.1.cell_misfit_ref, bf16[32,128]{1,0:T(8,128)(2,1)S(1)} %get-tuple-element.32.head_ref), custom_call_target="tpu_custom_call" | custom-call | flops 16777216 | bytes 524288 | tf_op jit(solution)/shard_map/latent_gradient/pallas_call | solution.py:370
  22.0 1.5 %collective-permute-done.5 = bf16[40,128]{1,0:T(8,128)(2,1)S(1)} collective-permute-done((bf16[40,128]{1,0:T(8,128)(2,1)S(1)}, bf16[40,128]{1,0:T(8,128)(2,1)S(1)}, u32[]{:S(2)}, u32[]{:S(2)}) %collective-permute-start.5) | collective-permute-done | bytes 10272 | tf_op jit(solution)/shard_map/ppermute | solution.py:245
  23.4 0.5 %collective-permute-start.6 = (bf16[40,128]{1,0:T(8,128)(2,1)S(1)}, bf16[40,128]{1,0:T(8,128)(2,1)S(1)}, u32[]{:S(2)}, u32[]{:S(2)}) collective-permute-start(bf16[40,128]{1,0:T(8,128)(2,1)S(1)} %convert_add_fusion.2), channel_id=1, source_target_pairs={{0,10},{1,11},{2,8},{3,9},{4,14},{5,15},{6,12},{7,13},{8,2},{9,3},... | collective-permute-start | bytes 30728 | tf_op jit(solution)/shard_map/ppermute | solution.py:245
  23.9 1.3 %collective-permute-start.7 = (bf16[40,128]{1,0:T(8,128)(2,1)S(1)}, bf16[40,128]{1,0:T(8,128)(2,1)S(1)}, u32[]{:S(2)}, u32[]{:S(2)}) collective-permute-start(bf16[40,128]{1,0:T(8,128)(2,1)S(1)} %convert_add_fusion.2), channel_id=1, source_target_pairs={{0,11},{1,10},{2,9},{3,8},{4,15},{5,14},{6,13},{7,12},{8,3},{9,2},... | collective-permute-start | bytes 30728 | tf_op jit(solution)/shard_map/ppermute | solution.py:245
  25.2 1.2 %collective-permute-start.8 = (bf16[40,128]{1,0:T(8,128)(2,1)S(1)}, bf16[40,128]{1,0:T(8,128)(2,1)S(1)}, u32[]{:S(2)}, u32[]{:S(2)}) collective-permute-start(bf16[40,128]{1,0:T(8,128)(2,1)S(1)} %convert_add_fusion.2), channel_id=1, source_target_pairs={{0,9},{1,8},{2,11},{3,10},{4,13},{5,12},{6,15},{7,14},{8,1},{9,0},... | collective-permute-start | bytes 30728 | tf_op jit(solution)/shard_map/ppermute | solution.py:245
  26.5 0.1 collective-permute-done.6
  26.6 1.3 %collective-permute-done.7 = bf16[40,128]{1,0:T(8,128)(2,1)S(1)} collective-permute-done((bf16[40,128]{1,0:T(8,128)(2,1)S(1)}, bf16[40,128]{1,0:T(8,128)(2,1)S(1)}, u32[]{:S(2)}, u32[]{:S(2)}) %collective-permute-start.7) | collective-permute-done | bytes 10272 | tf_op jit(solution)/shard_map/ppermute | solution.py:245
  27.9 0.4 %collective-permute-done.8 = bf16[40,128]{1,0:T(8,128)(2,1)S(1)} collective-permute-done((bf16[40,128]{1,0:T(8,128)(2,1)S(1)}, bf16[40,128]{1,0:T(8,128)(2,1)S(1)}, u32[]{:S(2)}, u32[]{:S(2)}) %collective-permute-start.8) | collective-permute-done | bytes 10272 | tf_op jit(solution)/shard_map/ppermute | solution.py:245
  28.4 0.6 %finish.1 = (f32[32,128]{1,0:T(8,128)}, f32[1,32]{1,0:T(1,128)}) custom-call(f32[40,128]{1,0:T(8,128)S(1)} %convert_add_fusion.1.mine_ref, f32[40,128]{1,0:T(8,128)S(1)} %convert_add_fusion.theirs_ref), custom_call_target="tpu_custom_call" | custom-call | tf_op jit(solution)/shard_map/finish/pallas_call | solution.py:386
  (5 shorter events, 0.1 us)
Async XLA Ops:
  0.6 0.7 %copy-start = (bf16[128,32]{0,1:T(8,128)(2,1)S(1)}, bf16[128,32]{0,1:T(8,128)(2,1)}, u32[]{:S(2)}) copy-start(bf16[128,32]{0,1:T(8,128)(2,1)} %param.9) | copy-start | bytes 24580
  4.6 8.6 %collective-permute-start = (bf16[256,128]{1,0:T(8,128)(2,1)S(1)}, bf16[256,128]{1,0:T(8,128)(2,1)S(1)}, u32[]{:S(2)}, u32[]{:S(2)}) collective-permute-start(bf16[256,128]{1,0:T(8,128)(2,1)S(1)} %get-tuple-element.21), channel_id=1, source_target_pairs={{0,1},{1,2},{2,3},{3,4},{4,5},{5,6},{6,7},{7,0},{8,9},{9,10},{10,1... | collective-permute-start | bytes 196616 | tf_op jit(solution)/shard_map/ppermute | solution.py:270
  7.7 5.7 %collective-permute-start.1 = (bf16[256,128]{1,0:T(8,128)(2,1)S(1)}, bf16[256,128]{1,0:T(8,128)(2,1)S(1)}, u32[]{:S(2)}, u32[]{:S(2)}) collective-permute-start(bf16[256,128]{1,0:T(8,128)(2,1)S(1)} %get-tuple-element.22), channel_id=1, source_target_pairs={{0,7},{1,0},{2,1},{3,2},{4,3},{5,4},{6,5},{7,6},{8,15},{9,8},{10,9... | collective-permute-start | bytes 196616 | tf_op jit(solution)/shard_map/ppermute | solution.py:270
  15.0 3.2 %collective-permute-start.3 = (bf16[40,128]{1,0:T(8,128)(2,1)S(1)}, bf16[40,128]{1,0:T(8,128)(2,1)S(1)}, u32[]{:S(2)}, u32[]{:S(2)}) collective-permute-start(bf16[40,128]{1,0:T(8,128)(2,1)S(1)} %convert_element_type.39), channel_id=1, source_target_pairs={{0,24},{1,25},{2,26},{3,27},{4,28},{5,29},{6,30},{7,31},{8,16},{9,... | collective-permute-start | bytes 30728 | tf_op jit(solution)/shard_map/ppermute | solution.py:245
  15.7 3.7 %collective-permute-start.2 = (bf16[40,128]{1,0:T(8,128)(2,1)S(1)}, bf16[40,128]{1,0:T(8,128)(2,1)S(1)}, u32[]{:S(2)}, u32[]{:S(2)}) collective-permute-start(bf16[40,128]{1,0:T(8,128)(2,1)S(1)} %convert_element_type.39), channel_id=1, source_target_pairs={{0,16},{1,17},{2,18},{3,19},{4,20},{5,21},{6,22},{7,23},{8,24},{9,... | collective-permute-start | bytes 30728 | tf_op jit(solution)/shard_map/ppermute | solution.py:245
  16.7 2.7 %collective-permute-start.4 = (bf16[40,128]{1,0:T(8,128)(2,1)S(1)}, bf16[40,128]{1,0:T(8,128)(2,1)S(1)}, u32[]{:S(2)}, u32[]{:S(2)}) collective-permute-start(bf16[40,128]{1,0:T(8,128)(2,1)S(1)} %convert_element_type.39), channel_id=1, source_target_pairs={{0,8},{1,9},{2,10},{3,11},{4,12},{5,13},{6,14},{7,15},{8,0},{9,1},... | collective-permute-start | bytes 30728 | tf_op jit(solution)/shard_map/ppermute | solution.py:245
  19.4 4.1 %collective-permute-start.5 = (bf16[40,128]{1,0:T(8,128)(2,1)S(1)}, bf16[40,128]{1,0:T(8,128)(2,1)S(1)}, u32[]{:S(2)}, u32[]{:S(2)}) collective-permute-start(bf16[40,128]{1,0:T(8,128)(2,1)S(1)} %add_add_fusion), channel_id=1, source_target_pairs={{0,12},{1,13},{2,14},{3,15},{4,8},{5,9},{6,10},{7,11},{8,4},{9,5},... | collective-permute-start | bytes 30728 | tf_op jit(solution)/shard_map/ppermute | solution.py:245
  23.4 3.2 %collective-permute-start.6 = (bf16[40,128]{1,0:T(8,128)(2,1)S(1)}, bf16[40,128]{1,0:T(8,128)(2,1)S(1)}, u32[]{:S(2)}, u32[]{:S(2)}) collective-permute-start(bf16[40,128]{1,0:T(8,128)(2,1)S(1)} %convert_add_fusion.2), channel_id=1, source_target_pairs={{0,10},{1,11},{2,8},{3,9},{4,14},{5,15},{6,12},{7,13},{8,2},{9,3},... | collective-permute-start | bytes 30728 | tf_op jit(solution)/shard_map/ppermute | solution.py:245
  23.9 4.0 %collective-permute-start.7 = (bf16[40,128]{1,0:T(8,128)(2,1)S(1)}, bf16[40,128]{1,0:T(8,128)(2,1)S(1)}, u32[]{:S(2)}, u32[]{:S(2)}) collective-permute-start(bf16[40,128]{1,0:T(8,128)(2,1)S(1)} %convert_add_fusion.2), channel_id=1, source_target_pairs={{0,11},{1,10},{2,9},{3,8},{4,15},{5,14},{6,13},{7,12},{8,3},{9,2},... | collective-permute-start | bytes 30728 | tf_op jit(solution)/shard_map/ppermute | solution.py:245
  25.2 3.1 %collective-permute-start.8 = (bf16[40,128]{1,0:T(8,128)(2,1)S(1)}, bf16[40,128]{1,0:T(8,128)(2,1)S(1)}, u32[]{:S(2)}, u32[]{:S(2)}) collective-permute-start(bf16[40,128]{1,0:T(8,128)(2,1)S(1)} %convert_add_fusion.2), channel_id=1, source_target_pairs={{0,9},{1,8},{2,11},{3,10},{4,13},{5,12},{6,15},{7,14},{8,1},{9,0},... | collective-permute-start | bytes 30728 | tf_op jit(solution)/shard_map/ppermute | solution.py:245
